TPU v7x, 128 devices: a whole 4x4x4 slice. The times are simulated.
128 devices in a mesh: grp: 16 (over y, x), tp: 8 (over z, core).
Axes of the slice: x: 4, y: 4, z: 4, core: 2. Of those that a mesh axis runs over, the one named last changes fastest.
Arguments:
- attn_out: bfloat16 [16384, 4096], P('grp', 'tp'), may hold values from -6 to 6
- o_proj: bfloat16 [4096, 8192], P(None, 'tp'), may hold values from -0.09375 to 0.09375
- residual: bfloat16 [16384, 8192], P('grp', 'tp'), may hold values from -80 to 80
- norm_gain: float32 [8192], P('tp'), may hold values from 0.5 to 1.5
- dest_group: int32 [16384, 1], P('grp'), may hold values from 0 to 15; in each aligned block of 1024 rows (0 to 1023, 1024 to 2047, ...) at most 128 rows name the same one
- accept_count: int32 [2048], P('grp'), may hold values from 1 to 8
- target_values: bfloat16 [16384, 512], P('grp'), may hold values from -6 to 6
- master: float32 [512, 8192], P('grp', 'tp'), may hold values from -0.0625 to 0.0625
- moment_one: float32 [512, 8192], P('grp', 'tp'), may hold values from -6 to 6
- moment_two: float32 [512, 8192], P('grp', 'tp'), may hold values from 0.25 to 4
Outputs:
- predictions: bfloat16 [32768, 512], P(('grp', 'tp'))
- new_master: float32 [512, 8192], P('grp', 'tp')
- new_moment_one: float32 [512, 8192], P('grp', 'tp')
- new_moment_two: float32 [512, 8192], P('grp', 'tp')
Inputs may be any that keep to these rules, and one draw needn't show every extreme that they name: `dest_group`: within the rows of one group no drafter shard is named by more than 128 rows, a bound that some block reaches.
All inputs are finite; a program needn't handle non-finite values.
Results may differ from a plain program's by a relative error of at most 0.0057.
Values may be sent and summed in bfloat16 or wider, within the bound.
A program may use at most 128 MiB of HBM per device.

v0:
```python
import math

import jax
import jax.numpy as jnp
from jax import lax
from jax.sharding import PartitionSpec as P

D = 8192
SPEC = 8


norm_eps = 1e-06
beta_one = 0.9
beta_two = 0.95
adam_eps = 1e-08
learn_rate = 0.01
decay_rate = 0.1
step_count = 10


def adam_update(master, moment_one, moment_two, gradient):
    first_moment = beta_one * moment_one + (1.0 - beta_one) * gradient
    second_moment = beta_two * moment_two + (1.0 - beta_two) * gradient * gradient
    update = (
        first_moment
        / (1.0 - beta_one**step_count)
        / (jnp.sqrt(second_moment / (1.0 - beta_two**step_count)) + adam_eps)
    )
    return (master - learn_rate * (update + decay_rate * master), first_moment, second_moment)


def rows_times(features, weight_slab):
    return lax.dot_general(
        features, weight_slab, (((1,), (1,)), ((), ())), preferred_element_type=jnp.float32
    )


def errors_times(errors, features):
    return lax.dot_general(
        errors, features, (((0,), (0,)), ((), ())), preferred_element_type=jnp.float32
    )


def masked_errors(weights, values, targets):
    return (weights.astype(jnp.float32)[:, None] * (values - targets.astype(jnp.float32))).astype(
        jnp.bfloat16
    )


def local(
    attn_out,
    o_proj,
    residual,
    norm_gain,
    dest_group,
    accept_count,
    target_values,
    master,
    moment_one,
    moment_two,
):
    group_count = lax.axis_size("grp")
    shard_count = lax.axis_size("tp")
    row_count = attn_out.shape[0]
    capacity = 2 * row_count // group_count
    slot_count = group_count * capacity
    portion = slot_count // shard_count
    tokens_all = row_count * group_count
    hidden = residual.astype(jnp.float32) + jnp.dot(
        lax.all_gather(attn_out, "tp", axis=1, tiled=True),
        o_proj,
        preferred_element_type=jnp.float32,
    )
    squares = lax.psum(jnp.sum(hidden * hidden, axis=1), "tp")
    scale_row = lax.rsqrt(squares / D + norm_eps)
    feature = (hidden * scale_row[:, None] * norm_gain[None, :]).astype(jnp.bfloat16)
    target_group = dest_group[:, 0]
    onehot = (target_group[:, None] == jnp.arange(group_count, dtype=jnp.int32)[None, :]).astype(
        jnp.int32
    )
    earlier = jnp.cumsum(onehot, axis=0) - onehot
    ranking = jnp.sum(earlier * onehot, axis=1)
    position = target_group * capacity + ranking
    accepted = (
        jnp.arange(row_count, dtype=jnp.int32) % SPEC < jnp.repeat(accept_count, SPEC)
    ).astype(jnp.bfloat16)
    send_features = (
        jnp.zeros((slot_count, feature.shape[1]), jnp.bfloat16).at[position].set(feature)
    )
    send_targets = (
        jnp.zeros((slot_count, target_values.shape[1]), jnp.bfloat16)
        .at[position]
        .set(target_values)
    )
    send_weights = jnp.zeros((slot_count,), jnp.bfloat16).at[position].set(accepted)
    weight_local = master.astype(jnp.bfloat16)
    features = lax.all_to_all(
        lax.all_to_all(send_features, "grp", split_axis=0, concat_axis=0, tiled=True),
        "tp",
        split_axis=0,
        concat_axis=1,
        tiled=True,
    )
    targets_all, weights_all = (
        lax.all_to_all(send_targets, "grp", split_axis=0, concat_axis=0, tiled=True),
        lax.all_to_all(send_weights, "grp", split_axis=0, concat_axis=0, tiled=True),
    )
    first_row = lax.axis_index("tp") * portion
    targets = lax.dynamic_slice_in_dim(targets_all, first_row, portion, 0)
    weights = lax.dynamic_slice_in_dim(weights_all, first_row, portion, 0)
    weight_wide = lax.all_gather(weight_local, "tp", axis=1, tiled=True)
    values = rows_times(features, lax.all_gather(weight_wide, "grp", axis=0, tiled=True))
    errors = masked_errors(weights, values, targets)
    grad_rows = lax.psum_scatter(
        errors_times(errors, features), "grp", scatter_dimension=0, tiled=True
    )
    gradient = lax.psum_scatter(grad_rows, "tp", scatter_dimension=1, tiled=True)
    gradient = gradient / math.sqrt(tokens_all)
    new_master, first_moment, second_moment = adam_update(master, moment_one, moment_two, gradient)
    return (values.astype(jnp.bfloat16), new_master, first_moment, second_moment)


def solution(mesh):
    in_specs = (
        P("grp", "tp"),
        P(None, "tp"),
        P("grp", "tp"),
        P("tp"),
        P("grp", None),
        P("grp"),
        P("grp", None),
        P("grp", "tp"),
        P("grp", "tp"),
        P("grp", "tp"),
    )
    out_specs = (P(("grp", "tp"), None), P("grp", "tp"), P("grp", "tp"), P("grp", "tp"))
    return jax.shard_map(local, mesh=mesh, in_specs=in_specs, out_specs=out_specs, check_vma=False)
```

profile of v0, /device:TPU:0, one launch (start us, length us, event | category | flops | bytes accessed | tf_op | source)
XLA Modules:
  0.0 431.5 jit_solution(18055685405329829330)
XLA Ops:
  7.2 0.0 all-gather.3.cloned.1.call-start
  7.2 0.7 all-gather.3.cloned.1.call-update
  7.9 0.0 all-gather.5.cloned.1.call-start
  7.9 0.9 convert_element_type.35
  8.9 15.5 %all_gather.10 = bf16[32,8192]{1,0:T(8,128)(2,1)} all-gather(bf16[32,1024]{1,0:T(8,128)(2,1)S(1)} %convert_element_type.35), channel_id=1, replica_groups=mesh['grp'=16,'tp'=8] {'tp'}, dimensions={1}, use_global_device_ids=true | all-gather | bytes 589824 | tf_op jit(solution)/shard_map/all_gather | solution.py:111
  24.4 0.0 all-gather.5.cloned.1.call-update
  24.4 0.7 broadcast_in_dim.10
  25.1 0.1 reshape.42
  25.2 0.7 fusion.10
  25.9 4.5 %reduce-window.6 = s32[16,8,128]{2,1,0:T(8,128)S(1)} reduce-window(s32[16,8,128]{2,1,0:T(8,128)S(1)} %fusion.10, s32[]{:T(128)} %constant.23.clone.1), window={size=1x1x128 pad=0_0x0_0x127_0}, to_apply=%region_0.0 | reduce-window | flops 2080768 | bytes 131076 | tf_op jit(solution)/shard_map/reduce-window
  30.4 0.1 slice.8
  30.5 0.1 copy.26
  30.7 0.1 copy.27
  30.7 0.1 broadcast_add_fusion
  30.8 0.7 fusion.9
  31.6 0.7 compare_select_fusion
  32.3 7.6 %scatter_custom_fusion.1 = bf16[2048]{0:T(1024)(128)(2,1)S(1)} fusion(s32[1024]{0:T(1024)S(1)} %bitcast.50, bf16[1024]{0:T(1024)(128)(2,1)S(1)} %fusion.15, bf16[]{:T(256)} %constant.21.clone.1), kind=kCustom, calls=%fused_computation.34 | custom fusion | bytes 4098 | tf_op jit(solution)/shard_map/scatter | solution.py:95
  39.9 0.6 copy.31
  40.5 7.0 %all-to-all-start.2 = ((bf16[16,128,1]{1,2,0:T(2,128)(2,1)}), bf16[16,128,1]{1,2,0:T(2,128)(2,1)S(1)}, u32[]{:S(2)}, u32[]{:S(2)}) async-start(bf16[16,128,1]{1,2,0:T(2,128)(2,1)} %copy.31), calls=%async_computation.2 | async-start | bytes 16384 | tf_op jit(solution)/shard_map/all_to_all | solution.py:106
  47.5 2.9 copy.28
  50.4 0.0 copy-start.3
  50.4 11.7 %all-gather.3.cloned.1.call-done = bf16[1024,4096]{1,0:T(8,128)(2,1)} async-done(((bf16[1024,512]{1,0:T(8,128)(2,1)}), bf16[1024,4096]{1,0:T(8,128)(2,1)}) %all-gather.3.cloned.1.call-update) | async-done | bytes 8388624 | tf_op jit(solution)/shard_map/all_gather | solution.py:70
  62.1 15.2 %multiply_reduce_fusion = (f32[1024]{0:T(1024)S(1)}, f32[1024,1024]{0,1:T(8,128)}) fusion(bf16[1024,1024]{0,1:T(8,128)(2,1)S(1)} %copy.28, bf16[1024,4096]{1,0:T(8,128)(2,1)} %all-gather.3.cloned.1.call-done, bf16[4096,1024]{1,0:T(8,128)(2,1)} %param.11), kind=kOutput, calls=%fused_computation.4 | convolution fusion | flops 8594127872 | bytes 23072768 | tf_op jit(solution)/shard_map/dot_general | solution.py:69
  77.3 13.7 %psum.7 = f32[1024]{0:T(1024)S(1)} all-reduce(f32[1024]{0:T(1024)S(1)} %get-tuple-element.7), channel_id=1, replica_groups=mesh['grp'=16,'tp'=8] {'tp'}, use_global_device_ids=true, to_apply=%region_4.5 | all-reduce | flops 1024 | bytes 8192 | tf_op jit(solution)/shard_map/psum | solution.py:74
  91.0 0.0 copy-done.3
  91.0 4.2 multiply_convert_fusion
  95.3 2.9 copy.29
  98.1 7.9 %scatter_custom_fusion = bf16[2048,1024]{1,0:T(8,128)(2,1)} fusion(s32[1024]{0:T(1024)S(1)} %bitcast.51, bf16[1024,1024]{1,0:T(8,128)(2,1)S(1)} %copy.29, bf16[]{:T(256)} %constant.21.clone.1), kind=kCustom, calls=%fused_computation.6 | custom fusion | bytes 4194306 | tf_op jit(solution)/shard_map/scatter | solution.py:88
  106.1 0.0 all-to-all-done.2
  106.1 76.0 %all_to_all.52 = bf16[16,128,1024]{2,1,0:T(8,128)(2,1)} all-to-all(bf16[16,128,1024]{2,1,0:T(8,128)(2,1)} %bitcast.39), channel_id=1, replica_groups=mesh['grp'=16,'tp'=8] {'grp'}, dimensions={0} | all-to-all | bytes 8388608 | tf_op jit(solution)/shard_map/all_to_all | solution.py:98
  182.1 4.6 %all-to-all-start.1 = ((bf16[8,256,1024]{2,1,0:T(8,128)(2,1)}), bf16[8,256,1024]{2,1,0:T(8,128)(2,1)}, u32[]{:S(2)}, u32[]{:S(2)}) async-start(bf16[8,256,1024]{2,1,0:T(8,128)(2,1)} %bitcast.38), calls=%async_computation.1 | async-start | bytes 8388608 | tf_op jit(solution)/shard_map/all_to_all | solution.py:97
  186.7 7.2 %scatter_custom_fusion.2 = bf16[2048,512]{1,0:T(8,128)(2,1)} fusion(s32[1024]{0:T(1024)S(1)} %bitcast.52, bf16[1024,512]{1,0:T(8,128)(2,1)} %param.16, bf16[]{:T(256)} %constant.21.clone.1), kind=kCustom, calls=%fused_computation.8 | custom fusion | bytes 2097664 | tf_op jit(solution)/shard_map/scatter | solution.py:93
  193.8 42.5 %all-to-all-done.1 = bf16[8,256,1024]{2,1,0:T(8,128)(2,1)} async-done(((bf16[8,256,1024]{2,1,0:T(8,128)(2,1)}), bf16[8,256,1024]{2,1,0:T(8,128)(2,1)}, u32[]{:S(2)}, u32[]{:S(2)}) %all-to-all-start.1) | async-done | bytes 4194336 | tf_op jit(solution)/shard_map/all_to_all | solution.py:97
  236.4 3.7 all-to-all-start.3
  240.1 0.3 reduce-scatter.3.cloned.1.call-start
  240.4 0.1 dynamic-slice_convert_fusion
  240.5 6.4 %copy.30 = bf16[256,8,1024]{0,2,1:T(8,128)(2,1)} copy(bf16[256,8,1024]{2,0,1:T(8,128)(2,1)} %bitcast.8) | data formatting | bytes 8388608 | tf_op jit(solution)/shard_map/all_to_all | solution.py:97
  246.9 7.7 %fusion.19 = (bf16[256,512]{1,0:T(8,128)(2,1)}, f32[256,512]{1,0:T(8,128)S(1)}) fusion(bf16[256,8192]{0,1:T(8,128)(2,1)} %bitcast.40, bf16[512,8192]{1,0:T(8,128)(2,1)} %all-gather.5.cloned.1.call-done), kind=kOutput, calls=%fused_computation.38 | convolution fusion | flops 2147614720 | bytes 13369344 | tf_op jit(solution)/shard_map/dot_general | solution.py:33
  254.7 17.3 %all-to-all-done.3 = bf16[16,128,512]{2,1,0:T(8,128)(2,1)S(1)} async-done(((bf16[16,128,512]{2,1,0:T(8,128)(2,1)}), bf16[16,128,512]{2,1,0:T(8,128)(2,1)S(1)}, u32[]{:S(2)}, u32[]{:S(2)}) %all-to-all-start.3) | async-done | bytes 2097184 | tf_op jit(solution)/shard_map/all_to_all | solution.py:105
  272.0 10.4 %fusion.4 = f32[512,8192]{1,0:T(8,128)} fusion(bf16[256,8192]{0,1:T(8,128)(2,1)} %bitcast.41, f32[256,512]{1,0:T(8,128)S(1)} %get-tuple-element.10, bf16[2048,512]{1,0:T(8,128)(2,1)S(1)} %bitcast.42, s32[]{:T(128)S(6)} %select_n.19, f32[256]{0:T(256)S(1)} %dynamic-slice_convert_fusion), kind=kOutput, calls=%fused_computation.11 | convolution fusion | flops 2148007936 | bytes 21758980 | tf_op jit(solution)/shard_map/dot_general | solution.py:39
  282.4 0.0 reduce-scatter.3.cloned.1.call-update
  282.4 0.0 reduce-scatter.5.cloned.1.call-start
  282.4 106.9 %reduce-scatter.3.cloned.1.call-done = f32[32,8192]{1,0:T(8,128)} async-done(((f32[512,8192]{1,0:T(8,128)}), f32[32,8192]{1,0:T(8,128)}) %reduce-scatter.3.cloned.1.call-update) | async-done | bytes 1048592 | tf_op jit(solution)/shard_map/reduce_scatter | solution.py:114
  389.3 0.0 reduce-scatter.5.cloned.1.call-update
  389.3 33.9 %reduce-scatter.5.cloned.1.call-done = f32[32,1024]{1,0:T(8,128)} async-done(((f32[32,8192]{1,0:T(8,128)}), f32[32,1024]{1,0:T(8,128)}) %reduce-scatter.5.cloned.1.call-update) | async-done | bytes 131088 | tf_op jit(solution)/shard_map/reduce_scatter | solution.py:117
  423.3 0.0 copy-done
  423.3 0.0 copy-done.1
  423.3 1.7 multiply_subtract_fusion
  (10 shorter events, 0.1 us)
Async XLA Ops:
  7.2 54.9 %all-gather.3.cloned.1.call-start = ((), (), s32[]{:S(2)}) async-start(), calls=%async_computation.6 | async-start | bytes 9437184 | tf_op jit(solution)/shard_map/all_gather | solution.py:70
  7.9 239.0 %all-gather.5.cloned.1.call-start = ((), (), s32[]{:S(2)}) async-start(), calls=%async_computation.7 | async-start | bytes 8912896 | tf_op jit(solution)/shard_map/all_gather | solution.py:112
  40.5 65.6 %all-to-all-start.2 = ((bf16[16,128,1]{1,2,0:T(2,128)(2,1)}), bf16[16,128,1]{1,2,0:T(2,128)(2,1)S(1)}, u32[]{:S(2)}, u32[]{:S(2)}) async-start(bf16[16,128,1]{1,2,0:T(2,128)(2,1)} %copy.31), calls=%async_computation.2 | async-start | bytes 16384 | tf_op jit(solution)/shard_map/all_to_all | solution.py:106
  50.4 40.6 %copy-start.3 = (f32[1024]{0:T(1024)S(1)}, f32[1024]{0:T(1024)}, u32[]{:S(2)}) copy-start(f32[1024]{0:T(1024)} %param.13) | copy-start | bytes 12292
  182.1 54.3 %all-to-all-start.1 = ((bf16[8,256,1024]{2,1,0:T(8,128)(2,1)}), bf16[8,256,1024]{2,1,0:T(8,128)(2,1)}, u32[]{:S(2)}, u32[]{:S(2)}) async-start(bf16[8,256,1024]{2,1,0:T(8,128)(2,1)} %bitcast.38), calls=%async_computation.1 | async-start | bytes 8388608 | tf_op jit(solution)/shard_map/all_to_all | solution.py:97
  236.4 35.6 %all-to-all-start.3 = ((bf16[16,128,512]{2,1,0:T(8,128)(2,1)}), bf16[16,128,512]{2,1,0:T(8,128)(2,1)S(1)}, u32[]{:S(2)}, u32[]{:S(2)}) async-start(bf16[16,128,512]{2,1,0:T(8,128)(2,1)} %bitcast.11), calls=%async_computation.3 | async-start | bytes 4194304 | tf_op jit(solution)/shard_map/all_to_all | solution.py:105
  240.1 149.2 %reduce-scatter.3.cloned.1.call-start = ((), (), s32[]{:S(2)}) async-start(), calls=%async_computation.8 | async-start | bytes 17825792 | tf_op jit(solution)/shard_map/reduce_scatter | solution.py:114
  282.3 140.9 %copy-start = (f32[32,1024]{1,0:T(8,128)S(1)}, f32[32,1024]{1,0:T(8,128)}, u32[]{:S(2)}) copy-start(f32[32,1024]{1,0:T(8,128)} %param.17) | copy-start | bytes 393220
  282.4 140.9 %copy-start.1 = (f32[32,1024]{1,0:T(8,128)S(1)}, f32[32,1024]{1,0:T(8,128)}, u32[]{:S(2)}) copy-start(f32[32,1024]{1,0:T(8,128)} %param.18) | copy-start | bytes 393220
  282.4 140.9 %copy-start.2 = (f32[32,1024]{1,0:T(8,128)S(1)}, f32[32,1024]{1,0:T(8,128)}, u32[]{:S(2)}) copy-start(f32[32,1024]{1,0:T(8,128)} %param.19) | copy-start | bytes 393220
  282.4 140.9 %reduce-scatter.5.cloned.1.call-start = ((), (), s32[]{:S(2)}) async-start(), calls=%async_computation.9 | async-start | bytes 1179648 | tf_op jit(solution)/shard_map/reduce_scatter | solution.py:117
Sparse Core Ops, SparseCore 0:
  9.7 52.3 all-gather.2
  64.2 110.6 all-gather.4
  282.5 106.7 reduce-scatter.2
  391.6 31.6 reduce-scatter.4
where the time goes:
time: 432 us
  waiting for transfers between devices  213 us (49%)
  blocking collectives  105 us (24%)
  local copies, waits for them, and re-layouts  36.6 us (8%)
  matrix products  33.3 us (8%)
  starting transfers between devices  15.7 us (4%)
  between operations  13.9 us (3%)
  other arithmetic  13.7 us (3%)
    reduce_scatter x1, waiting for transfers between devices, local(): lax.psum_scatter(errors_times(errors, features), 'grp', scatter_dimension...  107 us
    all_to_all x1, blocking collectives, local(): lax.all_to_all(send_features, 'grp', split_axis=0, concat_axis=0, tiled=T...  76 us
    all_to_all x1, waiting for transfers between devices, local(): lax.all_to_all(lax.all_to_all(send_features, 'grp', split_axis=0, concat_...  42.5 us
    reduce_scatter x1, waiting for transfers between devices, local(): lax.psum_scatter(grad_rows, 'tp', scatter_dimension=1, tiled=True)  33.9 us
    all_to_all x1, waiting for transfers between devices, local(): lax.all_to_all(send_targets, 'grp', split_axis=0, concat_axis=0, tiled=True)  17.3 us
    all_gather x1, blocking collectives, local(): weight_wide = lax.all_gather(weight_local, 'tp', axis=1, tiled=True)  15.5 us
    dot_general x1, matrix products, local(): jnp.dot(lax.all_gather(attn_out, 'tp', axis=1, tiled=True), o_proj, prefe...  15.2 us
    psum x1, blocking collectives, local(): squares = lax.psum(jnp.sum(hidden * hidden, axis=1), 'tp')  13.7 us
  transfers between devices with their start and end apart: 7, of which 5 were waited for; matrix products, arithmetic and copies ran while one was open for 17% of the time, Pallas kernels for 0%

commit v1 on v0

v1 whole, which is shorter than its diff:
```python
import math

import jax
import jax.numpy as jnp
from jax import lax
from jax.sharding import PartitionSpec as P

D = 8192
SPEC = 8


norm_eps = 1e-06
beta_one = 0.9
beta_two = 0.95
adam_eps = 1e-08
learn_rate = 0.01
decay_rate = 0.1
step_count = 10


def adam_update(master, moment_one, moment_two, gradient):
    first_moment = beta_one * moment_one + (1.0 - beta_one) * gradient
    second_moment = beta_two * moment_two + (1.0 - beta_two) * gradient * gradient
    update = (
        first_moment
        / (1.0 - beta_one**step_count)
        / (jnp.sqrt(second_moment / (1.0 - beta_two**step_count)) + adam_eps)
    )
    return (master - learn_rate * (update + decay_rate * master), first_moment, second_moment)


def local(
    attn_out,
    o_proj,
    residual,
    norm_gain,
    dest_group,
    accept_count,
    target_values,
    master,
    moment_one,
    moment_two,
):
    group_count = lax.axis_size("grp")
    shard_count = lax.axis_size("tp")
    row_count = attn_out.shape[0]
    capacity = 2 * row_count // group_count
    tokens_all = row_count * group_count
    g, t = lax.axis_index("grp"), lax.axis_index("tp")
    weight = lax.all_gather(master.astype(jnp.bfloat16), "grp", axis=0, tiled=True)
    hidden = residual.astype(jnp.float32) + jnp.dot(
        lax.all_gather(attn_out, "tp", axis=1, tiled=True),
        o_proj,
        preferred_element_type=jnp.float32,
    )
    squares = lax.psum(jnp.sum(hidden * hidden, axis=1), "tp")
    scale_row = lax.rsqrt(squares / D + norm_eps)
    feature = (hidden * scale_row[:, None] * norm_gain[None, :]).astype(jnp.bfloat16)
    partial = lax.dot_general(
        feature, weight, (((1,), (1,)), ((), ())), preferred_element_type=jnp.float32
    )
    values = lax.psum(partial, "tp")

    target_group = dest_group[:, 0]
    onehot = target_group[:, None] == jnp.arange(group_count, dtype=jnp.int32)[None, :]
    before = jnp.tril(jnp.ones((row_count, row_count), jnp.bfloat16), -1)
    earlier = jnp.dot(before, onehot.astype(jnp.bfloat16), preferred_element_type=jnp.float32)
    ranking = jnp.sum(jnp.where(onehot, earlier, 0.0), axis=1).astype(jnp.int32)
    accepted = (
        jnp.arange(row_count, dtype=jnp.int32) % SPEC < jnp.repeat(accept_count, SPEC)
    ).astype(jnp.float32)
    errors = (accepted[:, None] * (values - target_values.astype(jnp.float32))).astype(
        jnp.bfloat16
    )
    partial_grad = lax.dot_general(
        errors, feature, (((0,), (0,)), ((), ())), preferred_element_type=jnp.float32
    )
    gradient = lax.psum_scatter(partial_grad, "grp", scatter_dimension=0, tiled=True)
    gradient = gradient / math.sqrt(tokens_all)

    rows_out = values.astype(jnp.bfloat16)
    blocks = []
    for turn in range(2):
        dest = 2 * t + (turn + g) % 2
        spot = jnp.where(target_group == dest, ranking, -1)
        pick = (jnp.arange(capacity, dtype=jnp.int32)[:, None] == spot[None, :]).astype(jnp.bfloat16)
        block = jnp.dot(pick, rows_out, preferred_element_type=jnp.float32).astype(jnp.bfloat16)
        pairs = [
            (a * shard_count + b, (2 * b + (turn + a) % 2) * shard_count + a // 2)
            for a in range(group_count)
            for b in range(shard_count)
        ]
        blocks.append(lax.ppermute(block, ("grp", "tp"), pairs))
    first = jnp.where(g % 2 == 0, blocks[0], blocks[1])
    second = jnp.where(g % 2 == 0, blocks[1], blocks[0])
    predictions = jnp.concatenate([first, second], axis=0)
    new_master, first_moment, second_moment = adam_update(master, moment_one, moment_two, gradient)
    return (predictions, new_master, first_moment, second_moment)


def solution(mesh):
    in_specs = (
        P("grp", "tp"),
        P(None, "tp"),
        P("grp", "tp"),
        P("tp"),
        P("grp", None),
        P("grp"),
        P("grp", None),
        P("grp", "tp"),
        P("grp", "tp"),
        P("grp", "tp"),
    )
    out_specs = (P(("grp", "tp"), None), P("grp", "tp"), P("grp", "tp"), P("grp", "tp"))
    return jax.shard_map(local, mesh=mesh, in_specs=in_specs, out_specs=out_specs, check_vma=False)
```

time: 432 us -> 270 us (0.62)
  blocking collectives: 105 us -> 13.5 us
  local copies, waits for them, and re-layouts: 36.6 us -> 4.44 us
  starting transfers between devices: 15.7 us -> 2.51 us
  waiting for transfers between devices: 213 us -> 202 us
  matrix products: 33.3 us -> 25.7 us
  other arithmetic: 13.7 us -> 8.16 us
    all_to_all x1 -> x0, blocking collectives: 76 us -> none  [local(): lax.all_to_all(send_features, 'grp', split_axis=0, concat_axis=0, tiled=T...]
    reduce_scatter x2 -> x1, waiting for transfers between devices: 141 us -> 71 us  [local(): lax.psum_scatter(partial_grad, 'grp', scatter_dimension=0, tiled=True)]
    psum x0 -> x1, waiting for transfers between devices: none -> 64.6 us  [local(): values = lax.psum(partial, 'tp')]
    all_to_all x3 -> x0, waiting for transfers between devices: 59.8 us -> none  [the longest x1 42.5 us: local(): lax.all_to_all(lax.all_to_all(send_features, 'grp', split_axis=0, concat_...]
    all_gather x1, waiting for transfers between devices: 11.7 us -> 49.6 us  [local(): lax.all_gather(attn_out, 'tp', axis=1, tiled=True)]
    scatter x3 -> x0, local copies, waits for them, and re-layouts: 22.7 us -> none  [the longest x1 7.93 us: local(): jnp.zeros((slot_count, feature.shape[1]), jnp.bfloat16).at[position]]
    all_gather x1 -> x0, blocking collectives: 15.5 us -> none  [local(): weight_wide = lax.all_gather(weight_local, 'tp', axis=1, tiled=True)]
    all_to_all x3 -> x0, starting transfers between devices: 15.4 us -> none  [the longest x1 7.04 us: local(): lax.all_to_all(send_weights, 'grp', split_axis=0, concat_axis=0, tiled=True)]
  transfers between devices with their start and end apart: 7 -> 6, of which waited for: 5 -> 5; matrix products, arithmetic and copies ran while one was open for 17% -> 10% of each run, Pallas kernels for 0% -> 0%
where the time goes in v1:
time: 270 us
  waiting for transfers between devices  202 us (75%)
  matrix products  25.7 us (10%)
  between operations  13.9 us (5%)
  blocking collectives  13.5 us (5%)
  other arithmetic  8.16 us (3%)
  local copies, waits for them, and re-layouts  4.44 us (2%)
    reduce_scatter x1, waiting for transfers between devices, local(): lax.psum_scatter(partial_grad, 'grp', scatter_dimension=0, tiled=True)  71 us
    psum x1, waiting for transfers between devices, local(): values = lax.psum(partial, 'tp')  64.6 us
    all_gather x1, waiting for transfers between devices, local(): lax.all_gather(attn_out, 'tp', axis=1, tiled=True)  49.6 us
    dot_general x1, matrix products, local(): jnp.dot(lax.all_gather(attn_out, 'tp', axis=1, tiled=True), o_proj, prefe...  15.2 us
    psum x1, blocking collectives, local(): squares = lax.psum(jnp.sum(hidden * hidden, axis=1), 'tp')  13.5 us
    all_gather x1, waiting for transfers between devices, local(): lax.all_gather(master.astype(jnp.bfloat16), 'grp', axis=0, tiled=True)  12.5 us
  transfers between devices with their start and end apart: 6, of which 5 were waited for; matrix products, arithmetic and copies ran while one was open for 10% of the time, Pallas kernels for 0%

profile of v1, /device:TPU:0, one launch (start us, length us, event | category | flops | bytes accessed | tf_op | source)
XLA Modules:
  0.0 270.0 jit_solution(9110421296356798478)
XLA Ops:
  7.2 0.0 all-gather.3.cloned.1.call-start
  7.2 0.7 all-gather.3.cloned.1.call-update
  7.9 0.0 all-gather.5.cloned.1.call-start
  7.9 1.5 convert_element_type.47
  9.5 0.0 all-gather.5.cloned.1.call-update
  9.5 0.0 all-reduce.2.cloned.1.call-start
  9.6 2.9 %copy.15 = bf16[1024,1024]{0,1:T(8,128)(2,1)S(1)} copy(bf16[1024,1024]{1,0:T(8,128)(2,1)} %param.12) | data formatting | bytes 4194304 | tf_op args[2]
  12.4 0.0 copy-start.5
  12.4 49.6 %all-gather.3.cloned.1.call-done = bf16[1024,4096]{1,0:T(8,128)(2,1)} async-done(((bf16[1024,512]{1,0:T(8,128)(2,1)}), bf16[1024,4096]{1,0:T(8,128)(2,1)}) %all-gather.3.cloned.1.call-update) | async-done | bytes 8388624 | tf_op jit(solution)/shard_map/all_gather | solution.py:52
  62.1 15.2 %multiply_reduce_fusion = (f32[1024]{0:T(1024)S(1)}, f32[1024,1024]{0,1:T(8,128)}) fusion(bf16[1024,1024]{0,1:T(8,128)(2,1)S(1)} %copy.15, bf16[1024,4096]{1,0:T(8,128)(2,1)} %all-gather.3.cloned.1.call-done, bf16[4096,1024]{1,0:T(8,128)(2,1)} %param.11), kind=kOutput, calls=%fused_computation.1 | convolution fusion | flops 8594127872 | bytes 23072768 | tf_op jit(solution)/shard_map/dot_general | solution.py:51
  77.3 13.5 %psum.14 = f32[1024]{0:T(1024)S(1)} all-reduce(f32[1024]{0:T(1024)S(1)} %get-tuple-element.11), channel_id=1, replica_groups=mesh['grp'=16,'tp'=8] {'tp'}, use_global_device_ids=true, to_apply=%region_2.0 | all-reduce | flops 1024 | bytes 8192 | tf_op jit(solution)/shard_map/psum | solution.py:56
  90.8 0.0 copy-done.5
  90.8 4.1 %multiply_convert_fusion = bf16[1024,1024]{0,1:T(8,128)(2,1)} fusion(f32[1024,1024]{0,1:T(8,128)} %get-tuple-element.12, bf16[1024,1024]{0,1:T(8,128)(2,1)S(1)} %copy.15, f32[1024]{0:T(1024)S(1)} %copy-done.5, f32[1024]{0:T(1024)S(1)} %add_rsqrt_fusion), kind=kLoop, calls=%fused_computation | loop fusion | flops 5242880 | bytes 8396800 | tf_op jit(solution)/shard_map/convert_element_type | solution.py:58
  95.0 12.5 %all-gather.5.cloned.1.call-done = bf16[512,1024]{1,0:T(8,128)(2,1)} async-done(((bf16[32,1024]{1,0:T(8,128)(2,1)}), bf16[512,1024]{1,0:T(8,128)(2,1)}) %all-gather.5.cloned.1.call-update) | async-done | bytes 1048592 | tf_op jit(solution)/shard_map/all_gather | solution.py:50
  107.5 0.0 copy-start.8
  107.5 4.6 %fusion.26 = f32[1024,512]{1,0:T(8,128)} fusion(bf16[1024,1024]{0,1:T(8,128)(2,1)} %multiply_convert_fusion, bf16[512,1024]{1,0:T(8,128)(2,1)} %all-gather.5.cloned.1.call-done), kind=kOutput, calls=%fused_computation.43 | convolution fusion | flops 1073741824 | bytes 5242880 | tf_op jit(solution)/shard_map/dot_general | solution.py:59
  112.0 0.0 copy-start.7
  112.0 0.0 copy-start.1
  112.0 0.0 all-reduce.2.cloned.1.call-update
  112.1 0.0 reduce-scatter.2.cloned.1.call-start
  112.1 0.6 copy-done.7
  112.7 0.1 broadcast_in_dim.28
  112.8 0.1 reshape.45
  112.9 64.6 %all-reduce.2.cloned.1.call-done = f32[1024,512]{1,0:T(8,128)} async-done(((f32[1024,512]{1,0:T(8,128)}), f32[1024,512]{1,0:T(8,128)}) %all-reduce.2.cloned.1.call-update) | async-done | bytes 2097168 | tf_op jit(solution)/shard_map/psum | solution.py:62
  177.4 0.0 copy-done.8
  177.4 0.0 copy-done.1
  177.4 4.5 %fusion.10 = f32[512,1024]{1,0:T(8,128)} fusion(bf16[1024,1024]{0,1:T(8,128)(2,1)S(1)} %copy-done.1, f32[1024,512]{1,0:T(8,128)} %all-reduce.2.cloned.1.call-done, bf16[1024,512]{1,0:T(8,128)(2,1)S(1)} %copy-done.8, f32[1024]{0:T(1024)S(1)} %fusion.23), kind=kOutput, calls=%fused_computation.12 | convolution fusion | flops 1075838976 | bytes 7344128 | tf_op jit(solution)/shard_map/dot_general | solution.py:75
  181.9 0.0 copy-start.6
  182.0 0.0 reduce-scatter.2.cloned.1.call-update
  182.0 0.0 copy-start
  182.0 0.6 copy-done.6
  182.6 0.7 fusion.7
  183.4 0.2 copy-done
  183.6 0.3 convolution_convert_fusion.1
  183.9 0.0 copy-start.2
  183.9 0.0 copy-start.3
  183.9 0.0 copy-start.4
  183.9 0.8 collective-permute-start
  184.7 0.3 convolution_convert_fusion
  185.0 1.5 collective-permute-start.1
  186.6 0.0 collective-permute-done
  186.6 3.5 %collective-permute-done.1 = bf16[128,512]{1,0:T(8,128)(2,1)S(1)} collective-permute-done((bf16[128,512]{1,0:T(8,128)(2,1)S(1)}, bf16[128,512]{1,0:T(8,128)(2,1)S(1)}, u32[]{:S(2)}, u32[]{:S(2)}) %collective-permute-start.1) | collective-permute-done | bytes 131104 | tf_op jit(solution)/shard_map/ppermute | solution.py:93
  190.1 0.7 pad_maximum_fusion
  190.8 71.0 %reduce-scatter.2.cloned.1.call-done = f32[32,1024]{1,0:T(8,128)} async-done(((f32[512,1024]{1,0:T(8,128)}), f32[32,1024]{1,0:T(8,128)}) %reduce-scatter.2.cloned.1.call-update) | async-done | bytes 131088 | tf_op jit(solution)/shard_map/reduce_scatter | solution.py:78
  261.8 0.0 copy-done.2
  261.8 0.0 copy-done.3
  261.8 0.0 copy-done.4
  261.8 1.7 multiply_subtract_fusion
  (5 shorter events, 0.0 us)
Async XLA Ops:
  7.2 54.9 %all-gather.3.cloned.1.call-start = ((), (), s32[]{:S(2)}) async-start(), calls=%async_computation.1 | async-start | bytes 9437184 | tf_op jit(solution)/shard_map/all_gather | solution.py:52
  7.9 99.6 %all-gather.5.cloned.1.call-start = ((), (), s32[]{:S(2)}) async-start(), calls=%async_computation.2 | async-start | bytes 1114112 | tf_op jit(solution)/shard_map/all_gather | solution.py:50
  9.5 167.9 %all-reduce.2.cloned.1.call-start = ((), (), s32[]{:S(2)}) async-start(), calls=%async_computation.3 | async-start | bytes 4194304 | tf_op jit(solution)/shard_map/psum | solution.py:62
  12.4 78.4 %copy-start.5 = (f32[1024]{0:T(1024)S(1)}, f32[1024]{0:T(1024)}, u32[]{:S(2)}) copy-start(f32[1024]{0:T(1024)} %param.13) | copy-start | bytes 12292
  107.5 70.0 %copy-start.8 = (bf16[1024,512]{1,0:T(8,128)(2,1)S(1)}, bf16[1024,512]{1,0:T(8,128)(2,1)}, u32[]{:S(2)}) copy-start(bf16[1024,512]{1,0:T(8,128)(2,1)} %param.16) | copy-start | bytes 3145732
  112.0 0.7 copy-start.7
  112.0 65.4 %copy-start.1 = (bf16[1024,1024]{0,1:T(8,128)(2,1)S(1)}, bf16[1024,1024]{0,1:T(8,128)(2,1)}, u32[]{:S(2)}) copy-start(bf16[1024,1024]{0,1:T(8,128)(2,1)} %multiply_convert_fusion) | copy-start | bytes 6291460
  112.1 149.7 %reduce-scatter.2.cloned.1.call-start = ((), (), s32[]{:S(2)}) async-start(), calls=%async_computation.4 | async-start | bytes 2228224 | tf_op jit(solution)/shard_map/reduce_scatter | solution.py:78
  181.9 0.7 copy-start.6
  182.0 1.6 copy-start
  183.9 77.9 %copy-start.2 = (f32[32,1024]{1,0:T(8,128)S(1)}, f32[32,1024]{1,0:T(8,128)}, u32[]{:S(2)}) copy-start(f32[32,1024]{1,0:T(8,128)} %param.17) | copy-start | bytes 393220
  183.9 77.9 %copy-start.3 = (f32[32,1024]{1,0:T(8,128)S(1)}, f32[32,1024]{1,0:T(8,128)}, u32[]{:S(2)}) copy-start(f32[32,1024]{1,0:T(8,128)} %param.18) | copy-start | bytes 393220
  183.9 77.9 %copy-start.4 = (f32[32,1024]{1,0:T(8,128)S(1)}, f32[32,1024]{1,0:T(8,128)}, u32[]{:S(2)}) copy-start(f32[32,1024]{1,0:T(8,128)} %param.19) | copy-start | bytes 393220
  183.9 2.7 collective-permute-start
  185.0 5.0 %collective-permute-start.1 = (bf16[128,512]{1,0:T(8,128)(2,1)S(1)}, bf16[128,512]{1,0:T(8,128)(2,1)S(1)}, u32[]{:S(2)}, u32[]{:S(2)}) collective-permute-start(bf16[128,512]{1,0:T(8,128)(2,1)S(1)} %convolution_convert_fusion), channel_id=1, source_target_pairs={{0,8},{1,24},{2,40},{3,56},{4,72},{5,88},{6,104},{7,120},{8,0},{9,... | collective-permute-start | bytes 393224 | tf_op jit(solution)/shard_map/ppermute | solution.py:93
Sparse Core Ops, SparseCore 0:
  9.7 52.3 all-gather.2
  64.8 42.6 all-gather.4
  112.2 65.2 all-reduce.1
  182.1 79.6 reduce-scatter.1

commit v2 on v1

v2 whole, which is shorter than its diff:
```python
import functools
import math

import jax
import jax.numpy as jnp
from jax import lax
from jax.experimental import pallas as pl
from jax.experimental.pallas import tpu as pltpu
from jax.sharding import PartitionSpec as P

D = 8192
SPEC = 8


norm_eps = 1e-06
beta_one = 0.9
beta_two = 0.95
adam_eps = 1e-08
learn_rate = 0.01
decay_rate = 0.1
step_count = 10

MESH = pl.DeviceIdType.MESH
F32 = jnp.float32
BF16 = jnp.bfloat16

NZ = 4
CORES = 2
CHUNK = 256
EXTRA = 128


def adam_update(master, moment_one, moment_two, gradient):
    first_moment = beta_one * moment_one + (1.0 - beta_one) * gradient
    second_moment = beta_two * moment_two + (1.0 - beta_two) * gradient * gradient
    update = (
        first_moment
        / (1.0 - beta_one**step_count)
        / (jnp.sqrt(second_moment / (1.0 - beta_two**step_count)) + adam_eps)
    )
    return (master - learn_rate * (update + decay_rate * master), first_moment, second_moment)


def with_column(values, column):
    high = column.astype(BF16).astype(F32)
    low = column - high
    lane = lax.broadcasted_iota(jnp.int32, (values.shape[0], EXTRA), 1)
    extra = jnp.where(lane < EXTRA // 2, high, low)
    return values.astype(BF16), extra.astype(BF16)


def column_of(extra):
    extra = extra.astype(F32)
    return extra[:, 0:1] + extra[:, EXTRA // 2 : EXTRA // 2 + 1]


def kernel(
    attn,
    o_proj,
    residual,
    gain,
    dest,
    accept,
    target,
    master,
    pred,
    grad,
    a_all,
    w_own,
    res_own,
    tgt_own,
    mst_own,
    mst_all,
    u_all,
    part,
    pair_in,
    pair_sum,
    z_in,
    val_all,
    g_sum,
    g_out,
    g_in,
    p_out,
    spot,
    load_sem,
    ag_send,
    ag_recv,
    vs_send,
    vs_recv,
    m_send,
    m_recv,
    g_send,
    g_recv,
    p_send,
    p_recv,
):
    rows, width = attn.shape
    cols = o_proj.shape[1]
    kvw = target.shape[1]
    groups = lax.axis_size("grp")
    own_rows = kvw // groups
    capacity = 2 * rows // groups
    chunks = rows // CHUNK
    half = CHUNK // CORES
    sub = half // NZ
    g, t = lax.axis_index("grp"), lax.axis_index("tp")
    z, core = t // CORES, t % CORES
    other = 1 - core
    z_up, z_down, z_far = (z + 1) % NZ, (z + NZ - 1) % NZ, (z + 2) % NZ
    pred_shard = g // 2
    up, down, far = (g, z_up * CORES + core), (g, z_down * CORES + core), (g, z_far * CORES + core)
    sibling = (g, z * CORES + other)

    def is_self(j):
        return jnp.logical_and(t == pred_shard, g % 2 == j)

    sends = []

    def copy_to(src, dst, send_sem, recv_sem, device):
        copy = pltpu.make_async_remote_copy(
            src_ref=src,
            dst_ref=dst,
            send_sem=send_sem,
            recv_sem=recv_sem,
            device_id=device,
            device_id_type=MESH,
        )
        copy.start()
        sends.append(copy)

    def wait_for(dst, send_sem, recv_sem, device):
        pltpu.make_async_remote_copy(
            src_ref=dst,
            dst_ref=dst,
            send_sem=send_sem,
            recv_sem=recv_sem,
            device_id=device,
            device_id_type=MESH,
        ).wait_recv()

    def block(zz, cc, start, size):
        return a_all.at[
            pl.ds(start, size), pl.ds(pl.multiple_of((zz * CORES + cc) * width, width), width)
        ]

    loads = [
        pltpu.make_async_copy(master, mst_own, load_sem.at[0]),
        pltpu.make_async_copy(attn, block(z, core, 0, rows), load_sem.at[1]),
        pltpu.make_async_copy(residual, res_own, load_sem.at[2]),
        pltpu.make_async_copy(target, tgt_own, load_sem.at[3]),
    ]
    pieces = 4
    depth = o_proj.shape[0] // pieces
    for k in range(pieces):
        loads.append(
            pltpu.make_async_copy(
                o_proj.at[pl.ds(k * depth, depth)],
                w_own.at[pl.ds(k * depth, depth)],
                load_sem.at[4 + k],
            )
        )
    for load in loads:
        load.start()

    barrier = pltpu.get_barrier_semaphore()

    def greet(device):
        pl.semaphore_signal(barrier, inc=1, device_id=device, device_id_type=MESH)

    for device in (up, down, far, sibling):
        greet(device)
    for k in range(1, groups):
        greet(((g + k) % groups, t))
    for j in range(2):

        @pl.when(jnp.logical_not(is_self(j)))
        def _():
            greet((2 * t + j, pred_shard))

    pl.semaphore_wait(barrier, 4 + groups - 1 + 2 - (t == pred_shard).astype(jnp.int32))

    def send_own(i):
        start = i * CHUNK
        src = attn.at[pl.ds(start, CHUNK)]
        dst = block(z, core, start, CHUNK)
        copy_to(src, dst, ag_send.at[i, 0], ag_recv.at[i, 0], up)
        copy_to(src, dst, ag_send.at[i, 1], ag_recv.at[i, 1], down)
        copy_to(src, dst, ag_send.at[i, 2], ag_recv.at[i, 2], sibling)

    send_own(0)
    send_own(1)

    def mst_rows(gg):
        return mst_all.at[pl.ds(pl.multiple_of(gg * own_rows, own_rows), own_rows)]

    loads[0].wait()
    mst_rows(g)[...] = mst_own[...].astype(BF16)
    for k in range(1, groups):
        copy_to(mst_rows(g), mst_rows(g), m_send.at[k], m_recv.at[k], ((g + k) % groups, t))

    tile = 256
    for n in range(rows // tile):
        here = pl.ds(n * tile, tile)
        kinds = lax.broadcasted_iota(jnp.int32, (groups, rows), 0)
        onehot = (kinds == dest[...]).astype(F32).astype(BF16)
        earlier_rows = lax.broadcasted_iota(jnp.int32, (rows, tile), 0)
        these_rows = lax.broadcasted_iota(jnp.int32, (rows, tile), 1) + n * tile
        before = (earlier_rows < these_rows).astype(F32).astype(BF16)
        earlier = jnp.dot(onehot, before, preferred_element_type=F32)
        dest_here = dest[:, here]
        mine = lax.broadcasted_iota(jnp.int32, (groups, tile), 0) == dest_here
        rank = jnp.sum(jnp.where(mine, earlier, 0.0), axis=0, keepdims=True)
        spot[:, here] = dest_here * capacity + rank.astype(jnp.int32)

    def pass_on(i):
        start = i * CHUNK
        wait_for(block(z_down, core, start, CHUNK), ag_send.at[i, 0], ag_recv.at[i, 0], down)
        src = block(z_down, core, start, CHUNK // 2)
        copy_to(src, src, ag_send.at[i, 3], ag_recv.at[i, 3], up)
        src = block(z_down, core, start, CHUNK)
        copy_to(src, src, ag_send.at[i, 4], ag_recv.at[i, 4], sibling)
        wait_for(block(z_up, core, start, CHUNK), ag_send.at[i, 1], ag_recv.at[i, 1], up)
        src = block(z_up, core, start + CHUNK // 2, CHUNK // 2)
        copy_to(src, src, ag_send.at[i, 5], ag_recv.at[i, 5], down)
        src = block(z_up, core, start, CHUNK)
        copy_to(src, src, ag_send.at[i, 6], ag_recv.at[i, 6], sibling)

    def pass_far(i):
        start = i * CHUNK
        wait_for(block(z_far, core, start, CHUNK // 2), ag_send.at[i, 3], ag_recv.at[i, 3], down)
        wait_for(
            block(z_far, core, start + CHUNK // 2, CHUNK // 2), ag_send.at[i, 5], ag_recv.at[i, 5], up
        )
        src = block(z_far, core, start, CHUNK)
        copy_to(src, src, ag_send.at[i, 7], ag_recv.at[i, 7], sibling)

    def multiply(i):
        start = i * CHUNK
        wait_for(block(z, other, start, CHUNK), ag_send.at[i, 2], ag_recv.at[i, 2], sibling)
        wait_for(block(z_down, other, start, CHUNK), ag_send.at[i, 4], ag_recv.at[i, 4], sibling)
        wait_for(block(z_up, other, start, CHUNK), ag_send.at[i, 6], ag_recv.at[i, 6], sibling)
        wait_for(block(z_far, other, start, CHUNK), ag_send.at[i, 7], ag_recv.at[i, 7], sibling)
        if i == 0:
            for load in loads[1:]:
                load.wait()
            for k in range(1, groups):
                gg = (g + groups - k) % groups
                wait_for(mst_rows(gg), m_send.at[k], m_recv.at[k], (gg, t))
        here = pl.ds(start, CHUNK)

        def columns(n, squares):
            there = pl.ds(pl.multiple_of(n * 256, 256), 256)
            hidden = jnp.dot(a_all[here, :], w_own[:, there], preferred_element_type=F32)
            hidden = hidden + res_own[here, there].astype(F32)
            u_all[here, there] = (hidden * gain[:, there]).astype(BF16)
            squared = hidden * hidden
            return squares + squared[:, :128] + squared[:, 128:]

        squares = lax.fori_loop(0, cols // 256, columns, jnp.zeros((CHUNK, 128), F32))
        values = lax.dot_general(
            u_all[here, :],
            mst_all[...],
            (((1,), (1,)), ((), ())),
            preferred_element_type=F32,
        )
        main, extra = with_column(values, jnp.sum(squares, axis=1, keepdims=True))
        part[here, :kvw] = main
        part[here, kvw:] = extra
        src = part.at[pl.ds(pl.multiple_of(start + other * half, half), half)]
        copy_to(src, pair_in.at[i], vs_send.at[i, 0], vs_recv.at[i, 0], sibling)

    def add_pair(i):
        start = i * CHUNK
        wait_for(pair_in.at[i], vs_send.at[i, 0], vs_recv.at[i, 0], sibling)
        mine = pl.ds(pl.multiple_of(start + core * half, half), half)
        values = part[mine, :kvw].astype(F32) + pair_in[i, :, :kvw].astype(F32)
        column = column_of(part[mine, kvw:]) + column_of(pair_in[i, :, kvw:])
        main, extra = with_column(values, column)
        pair_sum[i, :, :kvw] = main
        pair_sum[i, :, kvw:] = extra
        for k in range(1, NZ):
            zz = (z + k) % NZ
            src = pair_sum.at[i, pl.ds(pl.multiple_of(zz * sub, sub), sub)]
            copy_to(
                src, z_in.at[i, k], vs_send.at[i, k], vs_recv.at[i, k], (g, zz * CORES + core)
            )

    def own_part(i, zz, cc):
        return pl.ds(pl.multiple_of(i * CHUNK + cc * half + zz * sub, sub), sub)

    def finish_values(i):
        mine = pl.ds(pl.multiple_of(z * sub, sub), sub)
        values = pair_sum[i, mine, :kvw].astype(F32)
        column = column_of(pair_sum[i, mine, kvw:])
        for k in range(1, NZ):
            zz = (z + NZ - k) % NZ
            wait_for(z_in.at[i, k], vs_send.at[i, k], vs_recv.at[i, k], (g, zz * CORES + core))
            values = values + z_in[i, k, :, :kvw].astype(F32)
            column = column + column_of(z_in[i, k, :, kvw:])
        scale = lax.rsqrt(column / D + norm_eps)
        main, extra = with_column(values * scale, scale)
        here = own_part(i, z, core)
        val_all[here, :kvw] = main
        val_all[here, kvw:] = extra
        for k in range(1, NZ):
            zz = (z + k) % NZ
            src = val_all.at[here]
            copy_to(
                src, src, vs_send.at[i, 3 + k], vs_recv.at[i, 3 + k], (g, zz * CORES + core)
            )

    def pass_values(i):
        for k in range(1, NZ):
            zz = (z + NZ - k) % NZ
            dst = val_all.at[own_part(i, zz, core)]
            wait_for(dst, vs_send.at[i, 3 + k], vs_recv.at[i, 3 + k], (g, zz * CORES + core))
        src = val_all.at[pl.ds(pl.multiple_of(i * CHUNK + core * half, half), half)]
        copy_to(src, src, vs_send.at[i, 7], vs_recv.at[i, 7], sibling)

    def add_gradient(i):
        start = i * CHUNK
        dst = val_all.at[pl.ds(pl.multiple_of(start + other * half, half), half)]
        wait_for(dst, vs_send.at[i, 7], vs_recv.at[i, 7], sibling)
        here = pl.ds(start, CHUNK)
        requests = accept.shape[1]
        row = lax.broadcasted_iota(jnp.int32, (CHUNK, requests), 0) + start
        request = lax.broadcasted_iota(jnp.int32, (CHUNK, requests), 1)
        taken = jnp.sum(
            jnp.where(row // SPEC == request, accept[...], 0).astype(F32), axis=1, keepdims=True
        )
        place = (lax.broadcasted_iota(jnp.int32, (CHUNK, 1), 0) % SPEC).astype(F32)
        weight = jnp.where(place < taken, column_of(val_all[here, kvw:]), 0.0)
        errors = weight * (val_all[here, :kvw].astype(F32) - tgt_own[here, :].astype(F32))
        product = lax.dot_general(
            errors.T.astype(BF16),
            u_all[here, :],
            (((1,), (0,)), ((), ())),
            preferred_element_type=F32,
        )
        if i == 0:
            g_sum[...] = product
        elif i < chunks - 1:
            g_sum[...] += product
        else:
            total = g_sum[...] + product
            g_sum[...] = total
            g_out[...] = total.astype(BF16)

    for it in range(chunks + 5):
        for stage, lag in (
            (pass_on, 0),
            (pass_far, 1),
            (add_pair, 2),
            (finish_values, 3),
            (pass_values, 4),
            (add_gradient, 5),
            (multiply, 1),
        ):
            i = it - lag
            if 0 <= i < chunks:
                stage(i)
            if stage is pass_on and 0 <= i + 2 < chunks and i >= 0:
                send_own(i + 2)

    def g_rows(gg):
        return pl.ds(pl.multiple_of(gg * own_rows, own_rows), own_rows)

    for k in range(1, groups):
        gg = (g + k) % groups
        copy_to(g_out.at[g_rows(gg)], g_in.at[k], g_send.at[k], g_recv.at[k], (gg, t))

    slot = lax.broadcasted_iota(jnp.int32, (2 * capacity, rows), 0) + 2 * t * capacity
    pick = (slot == spot[...]).astype(F32).astype(BF16)
    p_out[...] = jnp.dot(pick, val_all[:, :kvw], preferred_element_type=F32).astype(BF16)

    def pred_copy(j):
        return pltpu.make_async_remote_copy(
            src_ref=p_out.at[pl.ds(j * capacity, capacity)],
            dst_ref=pred.at[pl.ds(pl.multiple_of((g % 2) * capacity, capacity), capacity)],
            send_sem=p_send.at[j],
            recv_sem=p_recv.at[g % 2],
            device_id=(2 * t + j, pred_shard),
            device_id_type=MESH,
        )

    def pred_local(j):
        return pltpu.make_async_copy(
            p_out.at[pl.ds(j * capacity, capacity)],
            pred.at[pl.ds(j * capacity, capacity)],
            p_send.at[j],
        )

    for j in range(2):

        @pl.when(is_self(j))
        def _():
            pred_local(j).start()

        @pl.when(jnp.logical_not(is_self(j)))
        def _():
            pred_copy(j).start()

    total = g_sum[g_rows(g), :]
    for k in range(1, groups):
        gg = (g + groups - k) % groups
        wait_for(g_in.at[k], g_send.at[k], g_recv.at[k], (gg, t))
        total = total + g_in[k].astype(F32)
    grad[...] = total * (1.0 / math.sqrt(rows * groups))

    for j in range(2):

        @pl.when(is_self(j))
        def _():
            pred_local(j).wait()

        @pl.when(jnp.logical_not(is_self(j)))
        def _():
            pred_copy(j).wait_send()
            wait_for(
                pred.at[pl.ds(j * capacity, capacity)],
                p_send.at[j],
                p_recv.at[j],
                (2 * t + j, pred_shard),
            )

    for copy in sends:
        copy.wait_send()


def local(
    attn_out,
    o_proj,
    residual,
    norm_gain,
    dest_group,
    accept_count,
    target_values,
    master,
    moment_one,
    moment_two,
):
    groups = lax.axis_size("grp")
    rows, width = attn_out.shape
    depth, cols = o_proj.shape
    kvw = target_values.shape[1]
    own_rows = master.shape[0]
    chunks = rows // CHUNK
    half = CHUNK // CORES
    sub = half // NZ
    wide = kvw + EXTRA
    slots = 2 * (2 * rows // groups)
    any_spec = pl.BlockSpec(memory_space=pl.ANY)
    vmem_spec = pl.BlockSpec(memory_space=pltpu.VMEM)
    dma = pltpu.SemaphoreType.DMA
    pred, grad = pl.pallas_call(
        kernel,
        out_shape=(
            jax.ShapeDtypeStruct((slots, kvw), BF16),
            jax.ShapeDtypeStruct((own_rows, cols), F32),
        ),
        in_specs=[any_spec, any_spec, any_spec, vmem_spec, vmem_spec, vmem_spec, any_spec, any_spec],
        out_specs=(any_spec, vmem_spec),
        scratch_shapes=[
            pltpu.VMEM((rows, depth), BF16),
            pltpu.VMEM((depth, cols), BF16),
            pltpu.VMEM((rows, cols), BF16),
            pltpu.VMEM((rows, kvw), BF16),
            pltpu.VMEM((own_rows, cols), F32),
            pltpu.VMEM((kvw, cols), BF16),
            pltpu.VMEM((rows, cols), BF16),
            pltpu.VMEM((rows, wide), BF16),
            pltpu.VMEM((chunks, half, wide), BF16),
            pltpu.VMEM((chunks, half, wide), BF16),
            pltpu.VMEM((chunks, NZ, sub, wide), BF16),
            pltpu.VMEM((rows, wide), BF16),
            pltpu.VMEM((kvw, cols), F32),
            pltpu.VMEM((kvw, cols), BF16),
            pltpu.VMEM((groups, own_rows, cols), BF16),
            pltpu.VMEM((slots, kvw), BF16),
            pltpu.VMEM((1, rows), jnp.int32),
            dma((8,)),
            dma((chunks, 8)),
            dma((chunks, 8)),
            dma((chunks, 8)),
            dma((chunks, 8)),
            dma((groups,)),
            dma((groups,)),
            dma((groups,)),
            dma((groups,)),
            dma((2,)),
            dma((2,)),
        ],
        compiler_params=pltpu.CompilerParams(
            collective_id=0, has_side_effects=True, vmem_limit_bytes=56 * 2**20
        ),
        cost_estimate=pl.CostEstimate(
            flops=2 * rows * cols * (depth + 2 * kvw),
            bytes_accessed=2 * (depth * cols + rows * (cols + width + kvw)),
            transcendentals=0,
        ),
        name="step",
    )(
        attn_out,
        o_proj,
        residual,
        norm_gain.reshape(1, cols),
        dest_group.reshape(1, rows),
        accept_count.reshape(1, rows // SPEC),
        target_values,
        master,
    )
    new_master, first_moment, second_moment = adam_update(master, moment_one, moment_two, grad)
    return (pred, new_master, first_moment, second_moment)


def solution(mesh):
    in_specs = (
        P("grp", "tp"),
        P(None, "tp"),
        P("grp", "tp"),
        P("tp"),
        P("grp", None),
        P("grp"),
        P("grp", None),
        P("grp", "tp"),
        P("grp", "tp"),
        P("grp", "tp"),
    )
    out_specs = (P(("grp", "tp"), None), P("grp", "tp"), P("grp", "tp"), P("grp", "tp"))
    return jax.shard_map(local, mesh=mesh, in_specs=in_specs, out_specs=out_specs, check_vma=False)
```

time: 270 us -> 98.2 us (0.36)
  waiting for transfers between devices: 202 us -> 0 us
  Pallas kernels: 0 us -> 92.2 us
  matrix products: 25.7 us -> 0 us
  blocking collectives: 13.5 us -> 0 us
  between operations: 13.9 us -> 0.69 us
  other arithmetic: 8.16 us -> 1.7 us
  local copies, waits for them, and re-layouts: 4.44 us -> 1.68 us
    pallas_call x0 -> x1, Pallas kernels: none -> 92.2 us  [local(): pl.pallas_call(kernel, out_shape=(jax.ShapeDtypeStruct((slots, kvw), BF16...]
    reduce_scatter x1 -> x0, waiting for transfers between devices: 71 us -> none  [local(): lax.psum_scatter(partial_grad, 'grp', scatter_dimension=0, tiled=True)]
    psum x1 -> x0, waiting for transfers between devices: 64.6 us -> none  [local(): values = lax.psum(partial, 'tp')]
    all_gather x2 -> x0, waiting for transfers between devices: 62.2 us -> none  [the longest x1 49.6 us: local(): lax.all_gather(attn_out, 'tp', axis=1, tiled=True)]
    dot_general x6 -> x0, matrix products: 25.7 us -> none  [the longest x1 15.2 us: local(): jnp.dot(lax.all_gather(attn_out, 'tp', axis=1, tiled=True), o_proj, prefe...]
    psum x1 -> x0, blocking collectives: 13.5 us -> none  [local(): squares = lax.psum(jnp.sum(hidden * hidden, axis=1), 'tp')]
    convert_element_type x3 -> x0, other arithmetic: 5.7 us -> none  [the longest x1 4.15 us: local(): (hidden * scale_row[:, None] * norm_gain[None, :]).astype(jnp.bfloat16)]
    ppermute x2 -> x0, waiting for transfers between devices: 3.5 us -> none  [local(): blocks.append(lax.ppermute(block, ('grp', 'tp'), pairs))]
  transfers between devices with their start and end apart: 6 -> 0, of which waited for: 5 -> 0; matrix products, arithmetic and copies ran while one was open for 10% -> 0% of each run, Pallas kernels for 0% -> 0%
where the time goes in v2:
time: 98.2 us; the launch traced here: 96.3 us
  Pallas kernels  92.2 us (94%)
  other arithmetic  1.7 us (2%)
  local copies, waits for them, and re-layouts  1.68 us (2%)
    pallas_call x1, Pallas kernels, local(): pl.pallas_call(kernel, out_shape=(jax.ShapeDtypeStruct((slots, kvw), BF16...  92.2 us

profile of v2, /device:TPU:0, one launch (start us, length us, event | category | flops | bytes accessed | tf_op | source)
XLA Modules:
  0.0 96.3 jit_solution(13736824525935772596)
XLA Ops:
  0.6 0.0 copy-start
  0.6 0.0 copy-start.1
  0.7 0.0 copy-start.2
  0.7 92.2 %step.1 = (bf16[256,512]{1,0:T(8,128)(2,1)}, f32[32,1024]{1,0:T(8,128)}) custom-call(bf16[1024,512]{1,0:T(8,128)(2,1)} %attn.1, bf16[4096,1024]{1,0:T(8,128)(2,1)} %o_proj.1, bf16[1024,1024]{1,0:T(8,128)(2,1)} %residual.1, f32[1,1024]{1,0:T(1,128)} %bitcast.3, s32[1,1024]{1,0:T(1,128)} %bitcast.4, s32[1,128]{1,0:T(1,128)} %bitcast.5, ...), custom_call_target="tpu_custom_call" | custom-call | flops 10737418240 | bytes 12582912 | tf_op jit(solution)/shard_map/step/pallas_call | solution.py:455
  92.9 0.0 copy-done
  92.9 0.0 copy-done.1
  92.9 0.0 copy-done.2
  92.9 1.7 %multiply_subtract_fusion = (f32[32,1024]{1,0:T(8,128)}, f32[32,1024]{1,0:T(8,128)}, f32[32,1024]{1,0:T(8,128)}) fusion(f32[32,1024]{1,0:T(8,128)S(1)} %copy-done, f32[32,1024]{1,0:T(8,128)} %get-tuple-element.7, f32[32,1024]{1,0:T(8,128)S(1)} %copy-done.1, f32[32,1024]{1,0:T(8,128)S(1)} %copy-done.2), kind=kLoop, calls=%fused_computation.2 | loop fusion | flops 491520 | bytes 917504 | tf_op jit(solution)/shard_map/sub | solution.py:41
  94.6 1.7 %copy.15 = bf16[256,512]{1,0:T(8,128)(2,1)} copy(bf16[256,512]{1,0:T(8,128)(2,1)} %get-tuple-element.15) | data formatting | bytes 524288
Async XLA Ops:
  0.6 92.3 %copy-start = (f32[32,1024]{1,0:T(8,128)S(1)}, f32[32,1024]{1,0:T(8,128)}, u32[]{:S(2)}) copy-start(f32[32,1024]{1,0:T(8,128)} %master.1) | copy-start | bytes 393220
  0.6 92.3 %copy-start.1 = (f32[32,1024]{1,0:T(8,128)S(1)}, f32[32,1024]{1,0:T(8,128)}, u32[]{:S(2)}) copy-start(f32[32,1024]{1,0:T(8,128)} %param.18) | copy-start | bytes 393220
  0.7 92.3 %copy-start.2 = (f32[32,1024]{1,0:T(8,128)S(1)}, f32[32,1024]{1,0:T(8,128)}, u32[]{:S(2)}) copy-start(f32[32,1024]{1,0:T(8,128)} %param.19) | copy-start | bytes 393220

commit v3 on v2

v3 whole, which is shorter than its diff:
```python
import functools
import math

import jax
import jax.numpy as jnp
from jax import lax
from jax.experimental import pallas as pl
from jax.experimental.pallas import tpu as pltpu
from jax.sharding import PartitionSpec as P

D = 8192
SPEC = 8


norm_eps = 1e-06
beta_one = 0.9
beta_two = 0.95
adam_eps = 1e-08
learn_rate = 0.01
decay_rate = 0.1
step_count = 10

MESH = pl.DeviceIdType.MESH
F32 = jnp.float32
BF16 = jnp.bfloat16

NX, NY, NZ, CORES = 4, 4, 4, 2
SIZES = (384, 256, 256, 128)
STARTS = tuple(sum(SIZES[:i]) for i in range(len(SIZES)))
CHUNKS = len(SIZES)
LANES = 128
TILE = 256
OWN, UP, DOWN, FAR = range(4)


def adam_update(master, moment_one, moment_two, gradient):
    first_moment = beta_one * moment_one + (1.0 - beta_one) * gradient
    second_moment = beta_two * moment_two + (1.0 - beta_two) * gradient * gradient
    update = (
        first_moment
        / (1.0 - beta_one**step_count)
        / (jnp.sqrt(second_moment / (1.0 - beta_two**step_count)) + adam_eps)
    )
    return (master - learn_rate * (update + decay_rate * master), first_moment, second_moment)


def finish_kernel(pred, grad, master, one, two, pred_out, master_out, one_out, two_out):
    pred_out[...] = pred[...]
    master_out[...], one_out[...], two_out[...] = adam_update(
        master[...], one[...], two[...], grad[...]
    )


def kernel(
    attn,
    o_proj,
    residual,
    gain,
    dest,
    accept,
    target,
    master,
    pred,
    grad,
    a_all,
    w_own,
    res_own,
    tgt_own,
    mst_own,
    mst_all,
    u_all,
    near,
    part,
    pair_in,
    pair_sum,
    z_in,
    val_all,
    sq_out,
    sq_pair,
    sq_sum,
    sq_z,
    scales,
    g_sum,
    g_one_out,
    g_two_out,
    g_one_in,
    g_two_in,
    h_one,
    h_two,
    h_one_out,
    h_two_out,
    h_one_in,
    h_two_in,
    p_out,
    spot,
    load_sem,
    ag_send,
    ag_recv,
    vs_send,
    vs_recv,
    sq_send,
    sq_recv,
    m_send,
    m_recv,
    g_send,
    g_recv,
    p_send,
    p_recv,
):
    rows, width = attn.shape
    cols = o_proj.shape[1]
    kvw = target.shape[1]
    groups = NX * NY
    own_rows = kvw // groups
    side = cols // 2
    capacity = 2 * rows // groups
    g, t = lax.axis_index("grp"), lax.axis_index("tp")
    z, core = t // CORES, t % CORES
    y, x = g // NX, g % NX
    other = 1 - core

    def along_z(k):
        return (g, ((z + k) % NZ) * CORES + core)

    def along_x(k):
        return (y * NX + (x + k) % NX, t)

    def along_y(k):
        return (((y + k) % NY) * NX + x, t)

    up, down, far = along_z(1), along_z(NZ - 1), along_z(2)
    sibling = (g, z * CORES + other)

    def pred_to(j):
        turn = z + x if j == 0 else 2 * NY - z - x
        return ((y + turn) % NY) * NX + 2 * core + j, g // 2

    def pred_from(j):
        source = 2 * t + j
        source_y, source_x = source // NX, source % NX
        odd = x % 2
        turn = (y - source_y + NY) * (1 - odd) + (source_y - y + NY) * odd
        return source, ((turn - source_x + 2 * NZ) % NZ) * CORES + x // 2

    def is_self(device):
        return jnp.logical_and(device[0] == g, device[1] == t)

    sends = []

    def copy_to(src, dst, send_sem, recv_sem, device):
        copy = pltpu.make_async_remote_copy(
            src_ref=src,
            dst_ref=dst,
            send_sem=send_sem,
            recv_sem=recv_sem,
            device_id=device,
            device_id_type=MESH,
        )
        copy.start()
        sends.append(copy)

    def wait_for(dst, send_sem, recv_sem, device):
        pltpu.make_async_remote_copy(
            src_ref=dst,
            dst_ref=dst,
            send_sem=send_sem,
            recv_sem=recv_sem,
            device_id=device,
            device_id_type=MESH,
        ).wait_recv()

    def place(which, cc):
        return pl.ds(pl.multiple_of((which * CORES + cc) * width, width), width)

    def block(which, cc, start, size):
        return a_all.at[pl.ds(start, size), place(which, cc)]

    loads = [
        pltpu.make_async_copy(master, mst_own, load_sem.at[0]),
        pltpu.make_async_copy(attn, block(OWN, core, 0, rows), load_sem.at[1]),
        pltpu.make_async_copy(residual, res_own, load_sem.at[2]),
        pltpu.make_async_copy(target, tgt_own, load_sem.at[3]),
    ]
    for which, step in ((OWN, 0), (UP, 1), (DOWN, NZ - 1), (FAR, 2)):
        for cc in range(CORES):
            first = ((z + step) % NZ * CORES + cc) * width
            loads.append(
                pltpu.make_async_copy(
                    o_proj.at[pl.ds(pl.multiple_of(first, width), width)],
                    w_own.at[place(which, cc)],
                    load_sem.at[4 + which * CORES + cc],
                )
            )
    for load in loads:
        load.start()

    barrier = pltpu.get_barrier_semaphore()

    def greet(device):
        pl.semaphore_signal(barrier, inc=1, device_id=device, device_id_type=MESH)

    for k in range(1, NZ):
        greet(along_z(k))
        greet(along_x(k))
        greet(along_y(k))
    greet(sibling)
    expected = jnp.int32(3 * (NZ - 1) + 1)
    for j in range(2):

        @pl.when(jnp.logical_not(is_self(pred_from(j))))
        def _():
            greet(pred_from(j))

        expected = expected + 1 - is_self(pred_to(j)).astype(jnp.int32)
    pl.semaphore_wait(barrier, expected)

    def send_own(i):
        start, size = STARTS[i], SIZES[i]
        src = attn.at[pl.ds(start, size)]
        copy_to(src, block(DOWN, core, start, size), ag_send.at[i, 0], ag_recv.at[i, 0], up)
        copy_to(src, block(UP, core, start, size), ag_send.at[i, 1], ag_recv.at[i, 1], down)
        copy_to(src, block(OWN, core, start, size), ag_send.at[i, 2], ag_recv.at[i, 2], sibling)

    send_own(0)
    send_own(1)

    def mst_rows(first, count):
        return mst_all.at[pl.ds(pl.multiple_of(first * own_rows, own_rows), count * own_rows)]

    loads[0].wait()
    mst_rows(g, 1)[...] = mst_own[...].astype(BF16)
    for k in range(1, NX):
        copy_to(mst_rows(g, 1), mst_rows(g, 1), m_send.at[0, k], m_recv.at[0, k], along_x(k))

    for n in range(rows // TILE):
        here = pl.ds(n * TILE, TILE)
        kinds = lax.broadcasted_iota(jnp.int32, (groups, rows), 0)
        onehot = (kinds == dest[...]).astype(F32).astype(BF16)
        earlier_rows = lax.broadcasted_iota(jnp.int32, (rows, TILE), 0)
        these_rows = lax.broadcasted_iota(jnp.int32, (rows, TILE), 1) + n * TILE
        before = (earlier_rows < these_rows).astype(F32).astype(BF16)
        earlier = jnp.dot(onehot, before, preferred_element_type=F32)
        dest_here = dest[:, here]
        mine = lax.broadcasted_iota(jnp.int32, (groups, TILE), 0) == dest_here
        rank = jnp.sum(jnp.where(mine, earlier, 0.0), axis=0, keepdims=True)
        spot[:, here] = dest_here * capacity + rank.astype(jnp.int32)

    for k in range(1, NX):
        source = along_x(NX - k)
        wait_for(mst_rows(source[0], 1), m_send.at[0, k], m_recv.at[0, k], source)
    for k in range(1, NY):
        src = mst_rows(y * NX, NX)
        copy_to(src, src, m_send.at[1, k], m_recv.at[1, k], along_y(k))

    def pass_on(i):
        start, size = STARTS[i], SIZES[i]
        part_size = size // 2
        src = block(DOWN, core, start, size)
        wait_for(src, ag_send.at[i, 0], ag_recv.at[i, 0], down)
        copy_to(
            block(DOWN, core, start, part_size),
            block(FAR, core, start, part_size),
            ag_send.at[i, 3],
            ag_recv.at[i, 3],
            up,
        )
        copy_to(src, src, ag_send.at[i, 4], ag_recv.at[i, 4], sibling)
        src = block(UP, core, start, size)
        wait_for(src, ag_send.at[i, 1], ag_recv.at[i, 1], up)
        copy_to(
            block(UP, core, start + part_size, part_size),
            block(FAR, core, start + part_size, part_size),
            ag_send.at[i, 5],
            ag_recv.at[i, 5],
            down,
        )
        copy_to(src, src, ag_send.at[i, 6], ag_recv.at[i, 6], sibling)
        if i + 2 < CHUNKS:
            send_own(i + 2)

    def pass_far(i):
        start, size = STARTS[i], SIZES[i]
        part_size = size // 2
        wait_for(
            block(FAR, core, start, part_size), ag_send.at[i, 3], ag_recv.at[i, 3], down
        )
        wait_for(
            block(FAR, core, start + part_size, part_size), ag_send.at[i, 5], ag_recv.at[i, 5], up
        )
        src = block(FAR, core, start, size)
        copy_to(src, src, ag_send.at[i, 7], ag_recv.at[i, 7], sibling)

    def multiply(i):
        start, size = STARTS[i], SIZES[i]
        here = pl.ds(start, size)
        last = i == CHUNKS - 1
        depth = FAR * CORES * width
        for which, sem in ((OWN, 2), (DOWN, 4), (UP, 6)):
            wait_for(block(which, other, start, size), ag_send.at[i, sem], ag_recv.at[i, sem], sibling)
        if i == 0:
            for load in loads[1:]:
                load.wait()

        def near_columns(n, carry):
            there = pl.ds(pl.multiple_of(n * TILE, TILE), TILE)
            near[:, there] = jnp.dot(
                a_all[here, :depth], w_own[:depth, there], preferred_element_type=F32
            )
            return carry

        if last:
            lax.fori_loop(0, cols // TILE, near_columns, 0)
        wait_for(block(FAR, other, start, size), ag_send.at[i, 7], ag_recv.at[i, 7], sibling)

        def columns(n, squares):
            there = pl.ds(pl.multiple_of(n * TILE, TILE), TILE)
            if last:
                hidden = near[:, there] + jnp.dot(
                    a_all[here, depth:], w_own[depth:, there], preferred_element_type=F32
                )
            else:
                hidden = jnp.dot(a_all[here, :], w_own[:, there], preferred_element_type=F32)
            hidden = hidden + res_own[here, there].astype(F32)
            u_all[here, there] = (hidden * gain[:, there]).astype(BF16)
            squared = hidden * hidden
            return squares + squared[:, :LANES] + squared[:, LANES:]

        squares = lax.fori_loop(0, cols // TILE, columns, jnp.zeros((size, LANES), F32))
        total = jnp.sum(squares.T, axis=0, keepdims=True)
        sq_out[i, :, :size] = jnp.broadcast_to(total, (8, size))
        copy_to(sq_out.at[i], sq_pair.at[i], sq_send.at[i, 0], sq_recv.at[i, 0], sibling)
        if i == 0:
            for k in range(1, NY):
                source = (y + NY - k) % NY
                wait_for(
                    mst_rows(source * NX, NX), m_send.at[1, k], m_recv.at[1, k], along_y(NY - k)
                )
        part[here, :] = lax.dot_general(
            u_all[here, :],
            mst_all[...],
            (((1,), (1,)), ((), ())),
            preferred_element_type=F32,
        ).astype(BF16)
        half = size // CORES
        src = part.at[pl.ds(pl.multiple_of(start + other * half, half), half)]
        dst = pair_in.at[pl.ds(start // CORES, half)]
        copy_to(src, dst, vs_send.at[i, 0], vs_recv.at[i, 0], sibling)

    def add_pair(i):
        start, size = STARTS[i], SIZES[i]
        half = size // CORES
        sub = half // NZ
        first = start // CORES
        wait_for(sq_pair.at[i], sq_send.at[i, 0], sq_recv.at[i, 0], sibling)
        sq_sum[i] = sq_out[i] + sq_pair[i]
        for k in range(1, NZ):
            copy_to(sq_sum.at[i], sq_z.at[i, k], sq_send.at[i, k], sq_recv.at[i, k], along_z(k))
        here = pl.ds(first, half)
        wait_for(pair_in.at[here], vs_send.at[i, 0], vs_recv.at[i, 0], sibling)
        mine = pl.ds(pl.multiple_of(start + core * half, half), half)
        pair_sum[here, :] = (part[mine, :].astype(F32) + pair_in[here, :].astype(F32)).astype(BF16)
        for k in range(1, NZ):
            src = pair_sum.at[pl.ds(pl.multiple_of(first + (z + k) % NZ * sub, sub), sub)]
            dst = z_in.at[k, pl.ds(start // (CORES * NZ), sub)]
            copy_to(src, dst, vs_send.at[i, k], vs_recv.at[i, k], along_z(k))

    def own_part(i, zz):
        sub = SIZES[i] // (CORES * NZ)
        return pl.ds(pl.multiple_of(STARTS[i] + (core * NZ + zz) * sub, sub), sub)

    def finish_values(i):
        start, size = STARTS[i], SIZES[i]
        sub = size // (CORES * NZ)
        total = sq_sum[i]
        for k in range(1, NZ):
            wait_for(sq_z.at[i, k], sq_send.at[i, k], sq_recv.at[i, k], along_z(NZ - k))
            total = total + sq_z[i, k]
        scale = lax.rsqrt(total[:1, :size] / D + norm_eps)
        scales[pl.ds(start, size), :] = jnp.broadcast_to(scale, (LANES, size)).T
        mine = pl.ds(pl.multiple_of(start // CORES + z * sub, sub), sub)
        there = pl.ds(start // (CORES * NZ), sub)
        values = pair_sum[mine, :].astype(F32)
        for k in range(1, NZ):
            wait_for(z_in.at[k, there], vs_send.at[i, k], vs_recv.at[i, k], along_z(NZ - k))
            values = values + z_in[k, there, :].astype(F32)
        here = own_part(i, z)
        val_all[here, :] = (values * scales[here, :1]).astype(BF16)
        src = val_all.at[here]
        for k in range(1, NZ):
            copy_to(src, src, vs_send.at[i, 3 + k], vs_recv.at[i, 3 + k], along_z(k))

    def pass_values(i):
        half = SIZES[i] // CORES
        for k in range(1, NZ):
            dst = val_all.at[own_part(i, (z + NZ - k) % NZ)]
            wait_for(dst, vs_send.at[i, 3 + k], vs_recv.at[i, 3 + k], along_z(NZ - k))
        src = val_all.at[pl.ds(pl.multiple_of(STARTS[i] + core * half, half), half)]
        copy_to(src, src, vs_send.at[i, 7], vs_recv.at[i, 7], sibling)

    def send_first():
        for k in range(1, NX):
            src, dst = g_one_out.at[(x + k) % NX], g_one_in.at[k]
            copy_to(src, dst, g_send.at[0, k], g_recv.at[0, k], along_x(k))

    def send_second():
        for k in range(1, NY):
            src, dst = g_two_out.at[(y + k) % NY], g_two_in.at[k]
            copy_to(src, dst, g_send.at[1, k], g_recv.at[1, k], along_y(k))

    def add_gradient(i):
        start, size = STARTS[i], SIZES[i]
        half = size // CORES
        dst = val_all.at[pl.ds(pl.multiple_of(start + other * half, half), half)]
        wait_for(dst, vs_send.at[i, 7], vs_recv.at[i, 7], sibling)
        here = pl.ds(start, size)
        requests = accept.shape[1]
        row = lax.broadcasted_iota(jnp.int32, (size, requests), 0) + start
        request = lax.broadcasted_iota(jnp.int32, (size, requests), 1)
        taken = jnp.sum(
            jnp.where(row // SPEC == request, accept[...], 0).astype(F32), axis=1, keepdims=True
        )
        order = (lax.broadcasted_iota(jnp.int32, (size, 1), 0) % SPEC).astype(F32)
        weight = jnp.where(order < taken, scales[here, :1], 0.0)
        errors = weight * (val_all[here, :].astype(F32) - tgt_own[here, :].astype(F32))
        errors = errors.T.astype(BF16)
        for part_of, send in ((0, send_first), (1, send_second)):
            there = pl.ds(part_of * side, side)
            product = jnp.dot(errors, u_all[here, there], preferred_element_type=F32)
            if i > 0:
                product = product + g_sum[:, there]
            g_sum[:, there] = product
            if i == CHUNKS - 1:
                for yy in range(NY):
                    for xx in range(NX):
                        first = (yy * NX + xx) * own_rows
                        piece = product[first : first + own_rows].astype(BF16)
                        if part_of == 0:
                            g_one_out[xx, yy] = piece
                        else:
                            g_two_out[yy, xx] = piece
                send()

    for it in range(CHUNKS + 5):
        for stage, lag in (
            (pass_on, 0),
            (pass_far, 1),
            (add_pair, 2),
            (finish_values, 3),
            (pass_values, 4),
            (add_gradient, 5),
            (multiply, 1),
        ):
            if 0 <= it - lag < CHUNKS:
                stage(it - lag)

    slot = lax.broadcasted_iota(jnp.int32, (capacity, rows), 0)
    for j in range(2):
        pick = (slot + pred_to(j)[0] * capacity == spot[...]).astype(F32).astype(BF16)
        p_out[j] = jnp.dot(pick, val_all[...], preferred_element_type=F32).astype(BF16)

    def pred_copy(j):
        return pltpu.make_async_remote_copy(
            src_ref=p_out.at[j],
            dst_ref=pred.at[pl.ds(pl.multiple_of((g % 2) * capacity, capacity), capacity)],
            send_sem=p_send.at[j],
            recv_sem=p_recv.at[g % 2],
            device_id=pred_to(j),
            device_id_type=MESH,
        )

    def pred_local(j):
        return pltpu.make_async_copy(
            p_out.at[j],
            pred.at[pl.ds(pl.multiple_of((g % 2) * capacity, capacity), capacity)],
            p_send.at[j],
        )

    for j in range(2):

        @pl.when(is_self(pred_to(j)))
        def _():
            pred_local(j).start()

        @pl.when(jnp.logical_not(is_self(pred_to(j))))
        def _():
            pred_copy(j).start()

    for k in range(1, NX):
        wait_for(g_one_in.at[k], g_send.at[0, k], g_recv.at[0, k], along_x(NX - k))
    for yy in range(NY):
        mine = pl.ds(pl.multiple_of((yy * NX + x) * own_rows, own_rows), own_rows)
        total = g_sum[mine, :side]
        for k in range(1, NX):
            total = total + g_one_in[k, yy].astype(F32)
        h_one[yy] = total
        h_one_out[yy] = total.astype(BF16)
    for k in range(1, NY):
        src, dst = h_one_out.at[(y + k) % NY], h_one_in.at[k]
        copy_to(src, dst, g_send.at[2, k], g_recv.at[2, k], along_y(k))
    for k in range(1, NY):
        wait_for(g_two_in.at[k], g_send.at[1, k], g_recv.at[1, k], along_y(NY - k))
    for xx in range(NX):
        mine = pl.ds(pl.multiple_of((y * NX + xx) * own_rows, own_rows), own_rows)
        total = g_sum[mine, side:]
        for k in range(1, NY):
            total = total + g_two_in[k, xx].astype(F32)
        h_two[xx] = total
        h_two_out[xx] = total.astype(BF16)
    for k in range(1, NX):
        src, dst = h_two_out.at[(x + k) % NX], h_two_in.at[k]
        copy_to(src, dst, g_send.at[3, k], g_recv.at[3, k], along_x(k))
    norm = 1.0 / math.sqrt(rows * groups)
    total = h_one[y]
    for k in range(1, NY):
        wait_for(h_one_in.at[k], g_send.at[2, k], g_recv.at[2, k], along_y(NY - k))
        total = total + h_one_in[k].astype(F32)
    grad[:, :side] = total * norm
    total = h_two[x]
    for k in range(1, NX):
        wait_for(h_two_in.at[k], g_send.at[3, k], g_recv.at[3, k], along_x(NX - k))
        total = total + h_two_in[k].astype(F32)
    grad[:, side:] = total * norm

    for j in range(2):

        @pl.when(is_self(pred_to(j)))
        def _():
            pred_local(j).wait()

        @pl.when(jnp.logical_not(is_self(pred_to(j))))
        def _():
            pred_copy(j).wait_send()

        @pl.when(jnp.logical_not(is_self(pred_from(j))))
        def _():
            dst = pred.at[pl.ds(j * capacity, capacity)]
            wait_for(dst, p_send.at[j], p_recv.at[j], pred_from(j))

    for copy in sends:
        copy.wait_send()


def local(
    attn_out,
    o_proj,
    residual,
    norm_gain,
    dest_group,
    accept_count,
    target_values,
    master,
    moment_one,
    moment_two,
):
    groups = lax.axis_size("grp")
    rows, width = attn_out.shape
    depth, cols = o_proj.shape
    kvw = target_values.shape[1]
    own_rows = master.shape[0]
    capacity = 2 * rows // groups
    side = cols // 2
    largest = max(SIZES)
    any_spec = pl.BlockSpec(memory_space=pl.ANY)
    vmem_spec = pl.BlockSpec(memory_space=pltpu.VMEM)
    vmem = pltpu.VMEM
    dma = pltpu.SemaphoreType.DMA
    pred, grad = pl.pallas_call(
        kernel,
        out_shape=(
            jax.ShapeDtypeStruct((2 * capacity, kvw), BF16),
            jax.ShapeDtypeStruct((own_rows, cols), F32),
        ),
        in_specs=[any_spec, any_spec, any_spec, vmem_spec, vmem_spec, vmem_spec, any_spec, any_spec],
        out_specs=(any_spec, vmem_spec),
        scratch_shapes=[
            vmem((rows, depth), BF16),
            vmem((depth, cols), BF16),
            vmem((rows, cols), BF16),
            vmem((rows, kvw), BF16),
            vmem((own_rows, cols), F32),
            vmem((kvw, cols), BF16),
            vmem((rows, cols), BF16),
            vmem((SIZES[-1], cols), F32),
            vmem((rows, kvw), BF16),
            vmem((rows // CORES, kvw), BF16),
            vmem((rows // CORES, kvw), BF16),
            vmem((NZ, rows // (CORES * NZ), kvw), BF16),
            vmem((rows, kvw), BF16),
            vmem((CHUNKS, 8, largest), F32),
            vmem((CHUNKS, 8, largest), F32),
            vmem((CHUNKS, 8, largest), F32),
            vmem((CHUNKS, NZ, 8, largest), F32),
            vmem((rows, LANES), F32),
            vmem((kvw, cols), F32),
            vmem((NX, NY, own_rows, side), BF16),
            vmem((NY, NX, own_rows, side), BF16),
            vmem((NX, NY, own_rows, side), BF16),
            vmem((NY, NX, own_rows, side), BF16),
            vmem((NY, own_rows, side), F32),
            vmem((NX, own_rows, side), F32),
            vmem((NY, own_rows, side), BF16),
            vmem((NX, own_rows, side), BF16),
            vmem((NY, own_rows, side), BF16),
            vmem((NX, own_rows, side), BF16),
            vmem((2, capacity, kvw), BF16),
            vmem((1, rows), jnp.int32),
            dma((12,)),
            dma((CHUNKS, 8)),
            dma((CHUNKS, 8)),
            dma((CHUNKS, 8)),
            dma((CHUNKS, 8)),
            dma((CHUNKS, NZ)),
            dma((CHUNKS, NZ)),
            dma((2, NX)),
            dma((2, NX)),
            dma((4, NX)),
            dma((4, NX)),
            dma((2,)),
            dma((2,)),
        ],
        compiler_params=pltpu.CompilerParams(
            collective_id=0, has_side_effects=True, vmem_limit_bytes=56 * 2**20
        ),
        cost_estimate=pl.CostEstimate(
            flops=2 * rows * cols * (depth + 2 * kvw),
            bytes_accessed=2 * (depth * cols + rows * (cols + width + kvw)),
            transcendentals=0,
        ),
        name="step",
    )(
        attn_out,
        o_proj,
        residual,
        norm_gain.reshape(1, cols),
        dest_group.reshape(1, rows),
        accept_count.reshape(1, rows // SPEC),
        target_values,
        master,
    )
    own = jax.ShapeDtypeStruct((own_rows, cols), F32)
    return pl.pallas_call(
        finish_kernel,
        out_shape=(jax.ShapeDtypeStruct((2 * capacity, kvw), BF16), own, own, own),
        in_specs=[vmem_spec] * 5,
        out_specs=(vmem_spec,) * 4,
        cost_estimate=pl.CostEstimate(
            flops=16 * own_rows * cols, bytes_accessed=28 * own_rows * cols, transcendentals=0
        ),
        name="finish",
    )(pred, grad, master, moment_one, moment_two)


def solution(mesh):
    in_specs = (
        P("grp", "tp"),
        P(None, "tp"),
        P("grp", "tp"),
        P("tp"),
        P("grp", None),
        P("grp"),
        P("grp", None),
        P("grp", "tp"),
        P("grp", "tp"),
        P("grp", "tp"),
    )
    out_specs = (P(("grp", "tp"), None), P("grp", "tp"), P("grp", "tp"), P("grp", "tp"))
    return jax.shard_map(local, mesh=mesh, in_specs=in_specs, out_specs=out_specs, check_vma=False)
```

time: 98.2 us -> 85.9 us (0.87); the launches traced: 96.3 us -> 85.6 us
  Pallas kernels: 92.2 us -> 84.9 us
  other arithmetic: 1.7 us -> 0 us
  local copies, waits for them, and re-layouts: 1.68 us -> 0 us
    pallas_call x1 -> x2, Pallas kernels: 92.2 us -> 84.9 us  [the longest x1 82.9 us: local(): pl.pallas_call(kernel, out_shape=(jax.ShapeDtypeStruct((2 * capacity, kvw...]
    sub x1 -> x0, other arithmetic: 1.7 us -> none  [adam_update(): master - learn_rate * (update + decay_rate * master)]
    unnamed x7 -> x0, local copies, waits for them, and re-layouts: 1.68 us -> none
where the time goes in v3:
time: 85.9 us; the launch traced here: 85.6 us
  Pallas kernels  84.9 us (99%)
    pallas_call x1, Pallas kernels, local(): pl.pallas_call(kernel, out_shape=(jax.ShapeDtypeStruct((2 * capacity, kvw...  82.9 us
    pallas_call x1, Pallas kernels, local(): pl.pallas_call(finish_kernel, out_shape=(jax.ShapeDtypeStruct((2 * capaci...  2.06 us

profile of v3, /device:TPU:0, one launch (start us, length us, event | category | flops | bytes accessed | tf_op | source)
XLA Modules:
  0.0 85.6 jit_solution(9851381006607598120)
XLA Ops:
  0.6 82.9 %step.1 = (bf16[256,512]{1,0:T(8,128)(2,1)}, f32[32,1024]{1,0:T(8,128)}) custom-call(bf16[1024,512]{1,0:T(8,128)(2,1)} %attn.1, bf16[4096,1024]{1,0:T(8,128)(2,1)} %o_proj.1, bf16[1024,1024]{1,0:T(8,128)(2,1)} %residual.1, f32[1,1024]{1,0:T(1,128)} %bitcast.3, s32[1,1024]{1,0:T(1,128)} %bitcast.4, s32[1,128]{1,0:T(1,128)} %bitcast.5, ...), custom_call_target="tpu_custom_call" | custom-call | flops 10737418240 | bytes 12582912 | tf_op jit(solution)/shard_map/step/pallas_call | solution.py:567
  83.5 2.1 %finish.1 = (bf16[256,512]{1,0:T(8,128)(2,1)}, f32[32,1024]{1,0:T(8,128)}, f32[32,1024]{1,0:T(8,128)}, f32[32,1024]{1,0:T(8,128)}) custom-call(bf16[256,512]{1,0:T(8,128)(2,1)} %get-tuple-element.6.pred, f32[32,1024]{1,0:T(8,128)} %get-tuple-element.7.grad, f32[32,1024]{1,0:T(8,128)} %master.3, f32[32,1024]{1,0:T(8,128)} %one.1, f32[32,1024]{1,0:T(8,128)} %two.1), custom_call_target="tpu_custom_call" | custom-call | flops 524288 | bytes 917504 | tf_op jit(solution)/shard_map/finish/pallas_call | solution.py:641

commit v4 on v3

--- a/solution.py
+++ b/solution.py
@@ -25,7 +25,7 @@
 BF16 = jnp.bfloat16
 
 NX, NY, NZ, CORES = 4, 4, 4, 2
-SIZES = (384, 256, 256, 128)
+SIZES = (384, 384, 256)
 STARTS = tuple(sum(SIZES[:i]) for i in range(len(SIZES)))
 CHUNKS = len(SIZES)
 LANES = 128
@@ -80,6 +80,7 @@
     sq_sum,
     sq_z,
     scales,
+    live,
     g_sum,
     g_one_out,
     g_two_out,
@@ -245,6 +246,17 @@
         rank = jnp.sum(jnp.where(mine, earlier, 0.0), axis=0, keepdims=True)
         spot[:, here] = dest_here * capacity + rank.astype(jnp.int32)
 
+    requests = accept.shape[1]
+    for n in range(rows // TILE):
+        here = pl.ds(n * TILE, TILE)
+        row = lax.broadcasted_iota(jnp.int32, (TILE, requests), 0) + n * TILE
+        request = lax.broadcasted_iota(jnp.int32, (TILE, requests), 1)
+        taken = jnp.sum(
+            jnp.where(row // SPEC == request, accept[...], 0).astype(F32), axis=1, keepdims=True
+        )
+        order = (lax.broadcasted_iota(jnp.int32, (TILE, LANES), 0) % SPEC).astype(F32)
+        live[here, :] = jnp.where(order < taken, 1.0, 0.0)
+
     for k in range(1, NX):
         source = along_x(NX - k)
         wait_for(mst_rows(source[0], 1), m_send.at[0, k], m_recv.at[0, k], source)
@@ -290,42 +302,42 @@
         src = block(FAR, core, start, size)
         copy_to(src, src, ag_send.at[i, 7], ag_recv.at[i, 7], sibling)
 
-    def multiply(i):
+    depth = FAR * CORES * width
+
+    def multiply_near(i):
         start, size = STARTS[i], SIZES[i]
         here = pl.ds(start, size)
-        last = i == CHUNKS - 1
-        depth = FAR * CORES * width
         for which, sem in ((OWN, 2), (DOWN, 4), (UP, 6)):
             wait_for(block(which, other, start, size), ag_send.at[i, sem], ag_recv.at[i, sem], sibling)
         if i == 0:
             for load in loads[1:]:
                 load.wait()
 
-        def near_columns(n, carry):
+        def columns(n, carry):
             there = pl.ds(pl.multiple_of(n * TILE, TILE), TILE)
-            near[:, there] = jnp.dot(
+            near[i % 2, :size, there] = jnp.dot(
                 a_all[here, :depth], w_own[:depth, there], preferred_element_type=F32
             )
             return carry
 
-        if last:
-            lax.fori_loop(0, cols // TILE, near_columns, 0)
+        lax.fori_loop(0, cols // TILE, columns, 0, unroll=True)
+
+    def multiply_far(i):
+        start, size = STARTS[i], SIZES[i]
+        here = pl.ds(start, size)
         wait_for(block(FAR, other, start, size), ag_send.at[i, 7], ag_recv.at[i, 7], sibling)
 
         def columns(n, squares):
             there = pl.ds(pl.multiple_of(n * TILE, TILE), TILE)
-            if last:
-                hidden = near[:, there] + jnp.dot(
-                    a_all[here, depth:], w_own[depth:, there], preferred_element_type=F32
-                )
-            else:
-                hidden = jnp.dot(a_all[here, :], w_own[:, there], preferred_element_type=F32)
+            hidden = near[i % 2, :size, there] + jnp.dot(
+                a_all[here, depth:], w_own[depth:, there], preferred_element_type=F32
+            )
             hidden = hidden + res_own[here, there].astype(F32)
             u_all[here, there] = (hidden * gain[:, there]).astype(BF16)
             squared = hidden * hidden
             return squares + squared[:, :LANES] + squared[:, LANES:]
 
-        squares = lax.fori_loop(0, cols // TILE, columns, jnp.zeros((size, LANES), F32))
+        squares = lax.fori_loop(0, cols // TILE, columns, jnp.zeros((size, LANES), F32), unroll=True)
         total = jnp.sum(squares.T, axis=0, keepdims=True)
         sq_out[i, :, :size] = jnp.broadcast_to(total, (8, size))
         copy_to(sq_out.at[i], sq_pair.at[i], sq_send.at[i, 0], sq_recv.at[i, 0], sibling)
@@ -413,14 +425,7 @@
         dst = val_all.at[pl.ds(pl.multiple_of(start + other * half, half), half)]
         wait_for(dst, vs_send.at[i, 7], vs_recv.at[i, 7], sibling)
         here = pl.ds(start, size)
-        requests = accept.shape[1]
-        row = lax.broadcasted_iota(jnp.int32, (size, requests), 0) + start
-        request = lax.broadcasted_iota(jnp.int32, (size, requests), 1)
-        taken = jnp.sum(
-            jnp.where(row // SPEC == request, accept[...], 0).astype(F32), axis=1, keepdims=True
-        )
-        order = (lax.broadcasted_iota(jnp.int32, (size, 1), 0) % SPEC).astype(F32)
-        weight = jnp.where(order < taken, scales[here, :1], 0.0)
+        weight = live[here, :1] * scales[here, :1]
         errors = weight * (val_all[here, :].astype(F32) - tgt_own[here, :].astype(F32))
         errors = errors.T.astype(BF16)
         for part_of, send in ((0, send_first), (1, send_second)):
@@ -443,12 +448,13 @@
     for it in range(CHUNKS + 5):
         for stage, lag in (
             (pass_on, 0),
-            (pass_far, 1),
             (add_pair, 2),
             (finish_values, 3),
             (pass_values, 4),
+            (multiply_near, 0),
+            (pass_far, 1),
+            (multiply_far, 1),
             (add_gradient, 5),
-            (multiply, 1),
         ):
             if 0 <= it - lag < CHUNKS:
                 stage(it - lag)
@@ -484,6 +490,11 @@
         @pl.when(jnp.logical_not(is_self(pred_to(j))))
         def _():
             pred_copy(j).start()
+
+    early = len(sends) - NX - NY + 2
+    for copy in sends[:early]:
+        copy.wait_send()
+    del sends[:early]
 
     for k in range(1, NX):
         wait_for(g_one_in.at[k], g_send.at[0, k], g_recv.at[0, k], along_x(NX - k))
@@ -580,7 +591,7 @@
             vmem((own_rows, cols), F32),
             vmem((kvw, cols), BF16),
             vmem((rows, cols), BF16),
-            vmem((SIZES[-1], cols), F32),
+            vmem((2, largest, cols), F32),
             vmem((rows, kvw), BF16),
             vmem((rows // CORES, kvw), BF16),
             vmem((rows // CORES, kvw), BF16),
@@ -590,6 +601,7 @@
             vmem((CHUNKS, 8, largest), F32),
             vmem((CHUNKS, 8, largest), F32),
             vmem((CHUNKS, NZ, 8, largest), F32),
+            vmem((rows, LANES), F32),
             vmem((rows, LANES), F32),
             vmem((kvw, cols), F32),
             vmem((NX, NY, own_rows, side), BF16),

time: 85.9 us -> 80.7 us (0.939)
  Pallas kernels: 84.9 us -> 79.9 us
    pallas_call x1, Pallas kernels: 82.9 us -> 77.8 us  [local(): pl.pallas_call(kernel, out_shape=(jax.ShapeDtypeStruct((2 * capacity, kvw...]
where the time goes in v4:
time: 80.7 us; the launch traced here: 80.5 us
  Pallas kernels  79.9 us (99%)
    pallas_call x1, Pallas kernels, local(): pl.pallas_call(kernel, out_shape=(jax.ShapeDtypeStruct((2 * capacity, kvw...  77.8 us
    pallas_call x1, Pallas kernels, local(): pl.pallas_call(finish_kernel, out_shape=(jax.ShapeDtypeStruct((2 * capaci...  2.06 us

profile of v4, /device:TPU:0, one launch (start us, length us, event | category | flops | bytes accessed | tf_op | source)
XLA Modules:
  0.0 80.5 jit_solution(3285542367180134195)
XLA Ops:
  0.6 77.8 %step.1 = (bf16[256,512]{1,0:T(8,128)(2,1)}, f32[32,1024]{1,0:T(8,128)}) custom-call(bf16[1024,512]{1,0:T(8,128)(2,1)} %attn.1, bf16[4096,1024]{1,0:T(8,128)(2,1)} %o_proj.1, bf16[1024,1024]{1,0:T(8,128)(2,1)} %residual.1, f32[1,1024]{1,0:T(1,128)} %bitcast.3, s32[1,1024]{1,0:T(1,128)} %bitcast.4, s32[1,128]{1,0:T(1,128)} %bitcast.5, ...), custom_call_target="tpu_custom_call" | custom-call | flops 10737418240 | bytes 12582912 | tf_op jit(solution)/shard_map/step/pallas_call | solution.py:578
  78.5 2.1 %finish.1 = (bf16[256,512]{1,0:T(8,128)(2,1)}, f32[32,1024]{1,0:T(8,128)}, f32[32,1024]{1,0:T(8,128)}, f32[32,1024]{1,0:T(8,128)}) custom-call(bf16[256,512]{1,0:T(8,128)(2,1)} %get-tuple-element.6.pred, f32[32,1024]{1,0:T(8,128)} %get-tuple-element.7.grad, f32[32,1024]{1,0:T(8,128)} %master.3, f32[32,1024]{1,0:T(8,128)} %one.1, f32[32,1024]{1,0:T(8,128)} %two.1), custom_call_target="tpu_custom_call" | custom-call | flops 524288 | bytes 917504 | tf_op jit(solution)/shard_map/finish/pallas_call | solution.py:653

commit v5 on v4

--- a/solution.py
+++ b/solution.py
@@ -365,13 +365,13 @@
         first = start // CORES
         wait_for(sq_pair.at[i], sq_send.at[i, 0], sq_recv.at[i, 0], sibling)
         sq_sum[i] = sq_out[i] + sq_pair[i]
-        for k in range(1, NZ):
+        for k in (2, 1, 3):
             copy_to(sq_sum.at[i], sq_z.at[i, k], sq_send.at[i, k], sq_recv.at[i, k], along_z(k))
         here = pl.ds(first, half)
         wait_for(pair_in.at[here], vs_send.at[i, 0], vs_recv.at[i, 0], sibling)
         mine = pl.ds(pl.multiple_of(start + core * half, half), half)
         pair_sum[here, :] = (part[mine, :].astype(F32) + pair_in[here, :].astype(F32)).astype(BF16)
-        for k in range(1, NZ):
+        for k in (2, 1, 3):
             src = pair_sum.at[pl.ds(pl.multiple_of(first + (z + k) % NZ * sub, sub), sub)]
             dst = z_in.at[k, pl.ds(start // (CORES * NZ), sub)]
             copy_to(src, dst, vs_send.at[i, k], vs_recv.at[i, k], along_z(k))
@@ -384,7 +384,7 @@
         start, size = STARTS[i], SIZES[i]
         sub = size // (CORES * NZ)
         total = sq_sum[i]
-        for k in range(1, NZ):
+        for k in (2, 1, 3):
             wait_for(sq_z.at[i, k], sq_send.at[i, k], sq_recv.at[i, k], along_z(NZ - k))
             total = total + sq_z[i, k]
         scale = lax.rsqrt(total[:1, :size] / D + norm_eps)
@@ -392,18 +392,18 @@
         mine = pl.ds(pl.multiple_of(start // CORES + z * sub, sub), sub)
         there = pl.ds(start // (CORES * NZ), sub)
         values = pair_sum[mine, :].astype(F32)
-        for k in range(1, NZ):
+        for k in (2, 1, 3):
             wait_for(z_in.at[k, there], vs_send.at[i, k], vs_recv.at[i, k], along_z(NZ - k))
             values = values + z_in[k, there, :].astype(F32)
         here = own_part(i, z)
         val_all[here, :] = (values * scales[here, :1]).astype(BF16)
         src = val_all.at[here]
-        for k in range(1, NZ):
+        for k in (2, 1, 3):
             copy_to(src, src, vs_send.at[i, 3 + k], vs_recv.at[i, 3 + k], along_z(k))
 
     def pass_values(i):
         half = SIZES[i] // CORES
-        for k in range(1, NZ):
+        for k in (2, 1, 3):
             dst = val_all.at[own_part(i, (z + NZ - k) % NZ)]
             wait_for(dst, vs_send.at[i, 3 + k], vs_recv.at[i, 3 + k], along_z(NZ - k))
         src = val_all.at[pl.ds(pl.multiple_of(STARTS[i] + core * half, half), half)]
@@ -427,10 +427,12 @@
         here = pl.ds(start, size)
         weight = live[here, :1] * scales[here, :1]
         errors = weight * (val_all[here, :].astype(F32) - tgt_own[here, :].astype(F32))
-        errors = errors.T.astype(BF16)
+        errors = errors.astype(BF16)
         for part_of, send in ((0, send_first), (1, send_second)):
             there = pl.ds(part_of * side, side)
-            product = jnp.dot(errors, u_all[here, there], preferred_element_type=F32)
+            product = lax.dot_general(
+                errors, u_all[here, there], (((0,), (0,)), ((), ())), preferred_element_type=F32
+            )
             if i > 0:
                 product = product + g_sum[:, there]
             g_sum[:, there] = product

time: 80.7 us -> 80.5 us (level)
  no operation moved by 1% of the time
where the time goes in v5:
time: 80.5 us; the launch traced here: 79.8 us
  Pallas kernels  79.2 us (98%)
    pallas_call x1, Pallas kernels, local(): pl.pallas_call(kernel, out_shape=(jax.ShapeDtypeStruct((2 * capacity, kvw...  77.1 us
    pallas_call x1, Pallas kernels, local(): pl.pallas_call(finish_kernel, out_shape=(jax.ShapeDtypeStruct((2 * capaci...  2.06 us

profile of v5, /device:TPU:0, one launch (start us, length us, event | category | flops | bytes accessed | tf_op | source)
XLA Modules:
  0.0 79.8 jit_solution(10961712094660989429)
XLA Ops:
  0.6 77.1 %step.1 = (bf16[256,512]{1,0:T(8,128)(2,1)}, f32[32,1024]{1,0:T(8,128)}) custom-call(bf16[1024,512]{1,0:T(8,128)(2,1)} %attn.1, bf16[4096,1024]{1,0:T(8,128)(2,1)} %o_proj.1, bf16[1024,1024]{1,0:T(8,128)(2,1)} %residual.1, f32[1,1024]{1,0:T(1,128)} %bitcast.3, s32[1,1024]{1,0:T(1,128)} %bitcast.4, s32[1,128]{1,0:T(1,128)} %bitcast.5, ...), custom_call_target="tpu_custom_call" | custom-call | flops 10737418240 | bytes 12582912 | tf_op jit(solution)/shard_map/step/pallas_call | solution.py:580
  77.8 2.1 %finish.1 = (bf16[256,512]{1,0:T(8,128)(2,1)}, f32[32,1024]{1,0:T(8,128)}, f32[32,1024]{1,0:T(8,128)}, f32[32,1024]{1,0:T(8,128)}) custom-call(bf16[256,512]{1,0:T(8,128)(2,1)} %get-tuple-element.6.pred, f32[32,1024]{1,0:T(8,128)} %get-tuple-element.7.grad, f32[32,1024]{1,0:T(8,128)} %master.3, f32[32,1024]{1,0:T(8,128)} %one.1, f32[32,1024]{1,0:T(8,128)} %two.1), custom_call_target="tpu_custom_call" | custom-call | flops 524288 | bytes 917504 | tf_op jit(solution)/shard_map/finish/pallas_call | solution.py:655
